TPU v7x, 512 devices: a whole 4x8x8 slice. The times are simulated.
512 devices in a mesh: gx: 16 (over y_lo, x), gy: 32 (over y_hi, z, core).
Axes of the slice: x: 4, y: 8 (y_hi: 2, y_lo: 4; y = y_hi * 4 + y_lo), z: 8, core: 2. Of those that a mesh axis runs over, the one named last changes fastest.
Arguments:
- grid_field: float32 [128, 1024, 512], P('gy', 'gx'), may hold values from -6 to 6
- operator_blocks: float32 [16, 512, 4, 2, 1024], P('gx', 'gy'), may hold values from -0.75 to 0.75
- op_columns: int32 [16, 512, 4, 2], P('gx', 'gy'), may hold values from 0 to 3, as said below
- diag_inverse: float32 [16, 512, 2, 4, 1024], P('gx', 'gy'), may hold values from -3 to 3
- off_blocks: float32 [16, 512, 2, 3, 1024], P('gx', 'gy'), may hold values from -0.5 to 0.5
Outputs:
- advanced_field: float32 [128, 1024, 512], P('gy', 'gx')
Inputs may be any that keep to these rules, and one draw needn't show every extreme that they name: `op_columns`: for every group and block row, slot 0 names the block row itself and slot 1 another block row within two of it.
All inputs are finite; a program needn't handle non-finite values.
Results may differ from a plain program's by a relative error of at most 0.0001.
Values sent between devices are 32-bit elements; how exact they have to be, the bound alone decides.
No kernel may reach another device: no remote copies, remote signals or barrier semaphores. Data moves between devices by JAX's collectives and lax.ppermute only.
A program may use at most 64 MiB of HBM per device.

v0:
```python
import math

import jax
import jax.numpy as jnp
import ml_dtypes
import numpy as np
from jax import lax
from jax.experimental import pallas as pl
from jax.experimental.pallas import tpu as pltpu
from jax.sharding import PartitionSpec as P

NX = 512
NY = 1024
QUARTER = NY // 4
HALF = NX // 2
LANES = 128
SPAN = 16
BLOCK = 32
PART = SPAN // 2
VMEM_LIMIT = 24 * 1024 * 1024

f32 = jnp.float32
bf16 = jnp.bfloat16


def split_table(table):
    high = table.astype(ml_dtypes.bfloat16)
    low = (table - high.astype(np.float64)).astype(ml_dtypes.bfloat16)
    return high, low


def x_tables():
    parity = np.arange(2).reshape(2, 1, 1)
    x = np.arange(HALF).reshape(1, HALF, 1)
    k = 2 * np.arange(HALF // 2).reshape(1, 1, HALF // 2) + parity
    angle = (x * k % NX) * (2.0 * math.pi / NX)
    shape = (2, HALF, HALF // SPAN, PART)
    cosine = np.cos(angle).reshape(shape) / math.sqrt(NX)
    sine = np.sin(angle).reshape(shape) / math.sqrt(NX)
    forward = np.stack([cosine, -sine], axis=3)
    weight = np.where(k == 0, 1.0, 2.0).reshape(2, 1, HALF // SPAN, 1, PART)
    backward = (forward * weight).reshape(2, HALF, HALF).transpose(0, 2, 1)
    return split_table(forward.reshape(2, HALF, HALF)), split_table(backward)


def y_tables():
    q1 = np.arange(4).reshape(4, 1, 1)
    q2 = np.arange(QUARTER).reshape(1, QUARTER, 1)
    y2 = np.arange(QUARTER).reshape(1, 1, QUARTER)
    angle = ((q1 + 4 * q2) * y2 % NY) * (2.0 * math.pi / NY)
    cosine = np.cos(angle) / math.sqrt(NY)
    sine = np.sin(angle) / math.sqrt(NY)
    forward = np.concatenate([cosine, sine], axis=2)
    backward = np.concatenate([cosine.transpose(0, 2, 1), -sine.transpose(0, 2, 1)], axis=2)
    return split_table(forward), split_table(backward)


def split(values):
    high = values.astype(bf16)
    low = (values - high.astype(f32)).astype(bf16)
    return high, low


def mul(left, right):
    return jnp.dot(left, right, preferred_element_type=f32)


def lane_index(shape):
    return lax.broadcasted_iota(jnp.int32, shape, len(shape) - 1)


def swap_groups(parts):
    parts = list(parts)
    lane = lane_index(parts[0].shape)
    distance, reach = len(parts) // 2, LANES // 2
    while distance:
        first = (lane & reach) == 0
        for i in range(len(parts)):
            if not i & distance:
                a, b = parts[i], parts[i + distance]
                parts[i] = jnp.where(first, a, pltpu.roll(b, reach, 1))
                parts[i + distance] = jnp.where(first, pltpu.roll(a, LANES - reach, 1), b)
        distance, reach = distance // 2, reach // 2
    return parts


def turned(values):
    real = (lane_index(values.shape) & PART) == 0
    return jnp.where(real, pltpu.roll(values, LANES - PART, 1), -pltpu.roll(values, PART, 1))


def x_forward_kernel(grid_hbm, high_hbm, low_hbm, out_ref, grid_ref, high_ref, low_ref, sems):
    depth, lines, length = grid_ref.shape
    pairs = [(high_hbm, high_ref), (low_hbm, low_ref)]
    pairs += [(grid_hbm.at[z], grid_ref.at[z]) for z in range(depth)]
    copies = [
        pltpu.make_async_copy(source, target, sems.at[i])
        for i, (source, target) in enumerate(pairs)
    ]
    for copy in copies:
        copy.start()
    for copy in copies:
        copy.wait()
    near = grid_ref[:, :, :HALF].reshape(depth * lines, HALF)
    far = grid_ref[:, :, HALF:].reshape(depth * lines, HALF)
    sums = []
    for p, values in enumerate((near + far, near - far)):
        high, low = split(values)
        wide = mul(jnp.concatenate([high, low], axis=0), high_ref[p])
        sums.append(wide[: depth * lines] + (wide[depth * lines :] + mul(high, low_ref[p])))
    for a in range(HALF // LANES):
        columns = slice(a * LANES, (a + 1) * LANES)
        parts = [
            sums[p][z * lines : (z + 1) * lines, columns] for z in range(depth) for p in range(2)
        ]
        for b, part in enumerate(swap_groups(parts)):
            out_ref[8 * a + b] = part


def x_backward_kernel(in_ref, high_ref, low_ref, out_ref):
    depth, lines, length = out_ref.shape
    columns = [swap_groups([in_ref[8 * a + b] for b in range(8)]) for a in range(HALF // LANES)]
    results = []
    for p in range(2):
        rows = [
            jnp.concatenate([column[2 * z + p] for column in columns], axis=1)
            for z in range(depth)
        ]
        high, low = split(jnp.concatenate(rows, axis=0))
        wide = mul(jnp.concatenate([high, low], axis=0), high_ref[p])
        results.append(wide[: depth * lines] + (wide[depth * lines :] + mul(high, low_ref[p])))
    near, far = results
    out_ref[:, :, :HALF] = (near + far).reshape(depth, lines, HALF)
    out_ref[:, :, HALF:] = (near - far).reshape(depth, lines, HALF)


def quarter_product(values, high_table, low_table):
    both = jnp.concatenate([values, turned(values)], axis=0)
    high, low = split(both)
    wide = mul(high_table, jnp.concatenate([high, low], axis=1))
    return wide[:, :LANES] + (wide[:, LANES:] + mul(low_table, high))


def y_forward_kernel(in_ref, high_ref, low_ref, out_ref):
    a, b, c, d = [in_ref[i * QUARTER : (i + 1) * QUARTER, :] for i in range(4)]
    even_sum, even_difference = a + c, a - c
    odd_sum, odd_difference = b + d, turned(b - d)
    mixed = (
        even_sum + odd_sum,
        even_difference + odd_difference,
        even_sum - odd_sum,
        even_difference - odd_difference,
    )
    for q1 in range(4):
        result = quarter_product(mixed[q1], high_ref[q1], low_ref[q1])
        out_ref[:, 8 * q1 : 8 * q1 + 8, :] = result.reshape(QUARTER // 8, 8, LANES)


def y_backward_kernel(in_ref, high_ref, low_ref, out_ref):
    products = []
    for q1 in range(4):
        values = in_ref[:, 8 * q1 : 8 * q1 + 8, :].reshape(QUARTER, LANES)
        products.append(quarter_product(values, high_ref[q1], low_ref[q1]))
    a, b, c, d = products
    even_sum, even_difference = a + c, a - c
    odd_sum, odd_difference = b + d, turned(b - d)
    out_ref[0:QUARTER, :] = even_sum + odd_sum
    out_ref[QUARTER : 2 * QUARTER, :] = even_difference - odd_difference
    out_ref[2 * QUARTER : 3 * QUARTER, :] = even_sum - odd_sum
    out_ref[3 * QUARTER :, :] = even_difference + odd_difference


def spread_left(matrix):
    rest = matrix - matrix.astype(bf16).astype(f32)
    return jnp.concatenate([matrix, rest, matrix], axis=1).astype(bf16)


def three(matrix, right):
    high, low = split(right)
    return mul(spread_left(matrix), jnp.concatenate([high, high, low], axis=0))


def operator_kernel(columns_ref, blocks_ref, diag_ref, off_ref, out_ref, hold_ref):
    groups = blocks_ref.shape[0]
    lane = lane_index((BLOCK, LANES))
    row = lax.broadcasted_iota(jnp.int32, (BLOCK, LANES), 0)
    slab = lane % 32
    place = (row == (slab % 8) * 4 + lane // 32).astype(bf16)
    place = jnp.concatenate([place, place], axis=0)
    owner = slab // 8

    def rows(i):
        return slice(BLOCK * i, BLOCK * i + BLOCK)

    for i in range(4):
        for g in range(groups):
            matrix = blocks_ref[g, i].reshape(2 * BLOCK, BLOCK)
            rest = matrix - matrix.astype(bf16).astype(f32)
            spread = mul(jnp.concatenate([matrix, rest], axis=1).astype(bf16), place)
            hold_ref[g, rows(i), :] = jnp.where(
                owner == columns_ref[g, 2 * i], spread[:BLOCK], 0.0
            ) + jnp.where(owner == columns_ref[g, 2 * i + 1], spread[BLOCK:], 0.0)
    for half, order in ((0, (0, 1, 2, 3)), (1, (3, 2, 1, 0))):
        for step, i in enumerate(order):
            if step:
                last = order[step - 1]
                coupled = min(i, last)
                for g in range(groups):
                    hold_ref[g, rows(i), :] -= three(
                        off_ref[g, half, coupled], hold_ref[g, rows(last), :]
                    )
            for g in range(groups):
                hold_ref[g, rows(i), :] = three(diag_ref[g, half, i], hold_ref[g, rows(i), :])
    for g in range(groups):
        for level in range(4):
            high, low = split(hold_ref[g, pl.ds(level, 32, stride=4), :])
            out_ref[g, rows(level), 0:LANES] = high
            out_ref[g, rows(level), LANES:] = low


def apply_kernel(in_ref, operator_ref, out_ref):
    slabs = 32
    first = lane_index((LANES, LANES)) < 64
    for r in range(8):
        parts = [in_ref[pl.ds(8 * q1 + r, slabs, stride=32), :] for q1 in range(4)]
        values = jnp.concatenate(swap_groups(parts), axis=0)
        high, low = split(values)
        wide = jnp.concatenate(
            [
                jnp.concatenate([high, low], axis=1),
                jnp.concatenate([high, jnp.zeros_like(low)], axis=1),
            ],
            axis=0,
        )
        results = []
        for g in (2 * r, 2 * r + 1):
            both = mul(operator_ref[g], wide)
            results.append(both[:, :LANES] + both[:, LANES:])
        solved = jnp.where(first, results[0], results[1])
        parts = swap_groups([solved[32 * level : 32 * level + 32] for level in range(4)])
        for q1 in range(4):
            out_ref[pl.ds(8 * q1 + r, slabs, stride=32), :] = parts[q1]


def call(kernel, shape, *operands, dtype=f32, spaces=None, scratch=(), flops=0, limit=VMEM_LIMIT):
    spaces = spaces or [pltpu.VMEM] * len(operands)
    read = sum(math.prod(o.shape) * o.dtype.itemsize for o in operands)
    return pl.pallas_call(
        kernel,
        out_shape=jax.ShapeDtypeStruct(shape, dtype),
        in_specs=[pl.BlockSpec(memory_space=space) for space in spaces],
        out_specs=pl.BlockSpec(memory_space=pltpu.VMEM),
        scratch_shapes=scratch,
        cost_estimate=pl.CostEstimate(flops=flops, bytes_accessed=read, transcendentals=0),
        compiler_params=pltpu.CompilerParams(vmem_limit_bytes=limit),
    )(*operands)


def exchange(values, axis):
    return lax.all_to_all(values, axis, split_axis=0, concat_axis=0, tiled=True)


def body(grid_field, operator_blocks, op_columns, diag_inverse, off_blocks):
    depth, lines, length = grid_field.shape
    groups = operator_blocks.shape[1]
    forward_x, backward_x = x_tables()
    forward_y, backward_y = y_tables()
    square = (BLOCK, BLOCK)
    operator = call(
        operator_kernel,
        (groups, LANES, 2 * LANES),
        op_columns.reshape(groups, 8),
        operator_blocks.reshape((groups, 4, 2) + square),
        diag_inverse.reshape((groups, 2, 4) + square),
        off_blocks.reshape((groups, 2, 3) + square),
        dtype=bf16,
        spaces=[pltpu.SMEM] + [pltpu.VMEM] * 3,
        scratch=[pltpu.VMEM((groups, LANES, LANES), f32)],
        flops=2 * 3 * groups * 22 * BLOCK * BLOCK * LANES,
    )
    x_flops = 2 * 3 * depth * lines * length * HALF
    y_flops = 2 * 3 * 4 * QUARTER * 2 * QUARTER * LANES
    values = call(
        x_forward_kernel,
        (16, lines, LANES),
        grid_field,
        *forward_x,
        spaces=[pl.ANY] * 3,
        scratch=[
            pltpu.VMEM(grid_field.shape, f32),
            pltpu.VMEM((2, HALF, HALF), bf16),
            pltpu.VMEM((2, HALF, HALF), bf16),
            pltpu.SemaphoreType.DMA((2 + depth,)),
        ],
        flops=x_flops,
        limit=56 * 1024 * 1024,
    )
    values = exchange(values, "gx").reshape(NY, LANES)
    values = call(y_forward_kernel, (32, 32, LANES), values, *forward_y, flops=y_flops)
    values = exchange(values, "gy").reshape(NY, LANES)
    values = call(
        apply_kernel, (NY, LANES), values, operator, flops=2 * 3 * groups * LANES * LANES * LANES
    )
    values = exchange(values.reshape(32, 32, LANES), "gy")
    values = call(y_backward_kernel, (NY, LANES), values, *backward_y, flops=y_flops)
    values = exchange(values.reshape(16, lines, LANES), "gx")
    return call(
        x_backward_kernel, (depth, lines, length), values, *backward_x, flops=x_flops
    )


def solution(mesh):
    placed = (
        P("gy", "gx", None),
        P("gx", "gy", None, None, None),
        P("gx", "gy", None, None),
        P("gx", "gy", None, None, None),
        P("gx", "gy", None, None, None),
    )
    return jax.shard_map(
        body, mesh=mesh, in_specs=placed, out_specs=P("gy", "gx", None), check_vma=False
    )
```

profile of v0, /device:TPU:1, one launch (start us, length us, event | category | flops | bytes accessed | tf_op | source)
XLA Modules:
  0.0 111.3 jit_solution(5449307364148516474)
XLA Ops:
  0.0 0.0 copy-start.4
  0.0 0.0 copy-start.5
  0.0 3.0 %shard_map.127 = f32[16,64,128]{2,1,0:T(8,128)} custom-call(f32[4,64,512]{2,1,0:T(8,128)} %grid_hbm.1, bf16[2,256,256]{2,1,0:T(8,128)(2,1)} %constant.16.clone.high_hbm, bf16[2,256,256]{2,1,0:T(8,128)(2,1)} %constant.17.clone.low_hbm), custom_call_target="tpu_custom_call" | custom-call | flops 201326592 | bytes 1048576 | tf_op jit(solution)/shard_map/pallas_call | solution.py:248
  3.0 20.4 %all_to_all.20 = f32[16,64,128]{2,1,0:T(8,128)S(1)} all-to-all(f32[16,64,128]{2,1,0:T(8,128)} %shard_map.127), channel_id=1, replica_groups=mesh['gx'=16,'gy'=32] {'gx'}, dimensions={0} | all-to-all | bytes 1048576 | tf_op jit(solution)/shard_map/all_to_all | solution.py:260
  23.4 0.0 copy-done.4
  23.4 0.0 copy-done.5
  23.4 0.0 copy-start.10
  23.4 1.6 %shard_map.128 = f32[32,32,128]{2,1,0:T(8,128)} custom-call(f32[1024,128]{1,0:T(8,128)S(1)} %bitcast.7, bf16[4,256,512]{2,1,0:T(8,128)(2,1)S(1)} %copy-done.4, bf16[4,256,512]{2,1,0:T(8,128)(2,1)S(1)} %copy-done.5), custom_call_target="tpu_custom_call" | custom-call | flops 402653184 | bytes 2621440 | tf_op jit(solution)/shard_map/pallas_call | solution.py:248
  25.0 17.0 %all-to-all-start.1 = ((f32[32,32,128]{2,1,0:T(8,128)}), f32[32,32,128]{2,1,0:T(8,128)}, u32[]{:S(2)}, u32[]{:S(2)}) async-start(f32[32,32,128]{2,1,0:T(8,128)} %shard_map.128), calls=%async_computation.1 | async-start | bytes 1048576 | tf_op jit(solution)/shard_map/all_to_all | solution.py:260
  42.1 0.0 copy-done.10
  42.1 0.0 copy-start.8
  42.1 0.7 reshape.32
  42.8 0.0 copy-start.9
  42.8 1.4 %copy.18.off_ref = f32[16,2,3,32,32]{4,3,2,1,0:T(8,128)} copy(f32[16,2,3,32,32]{4,3,1,2,0:T(8,128)S(1)} %reshape.32) | data formatting | bytes 786432 | tf_op jit(solution)/shard_map/reshape | solution.py:275
  44.2 0.0 copy-done.8
  44.2 0.0 copy-start.11
  44.2 0.9 reshape.27.blocks_ref
  45.0 0.0 copy-done.9
  45.0 2.0 %reshape.28.diag_ref = f32[16,2,4,32,32]{4,3,2,1,0:T(8,128)} reshape(f32[1,16,2,4,1024]{4,3,2,1,0:T(4,128)S(1)} %copy-done.9) | data formatting | bytes 1048576 | tf_op jit(solution)/shard_map/reshape | solution.py:274
  47.1 0.0 copy-done.11
  47.1 0.1 copy.17.columns_ref
  47.2 0.0 copy-start
  47.2 1.6 %copy-done = f32[16,2,4,32,32]{4,3,2,1,0:T(8,128)S(1)} copy-done((f32[16,2,4,32,32]{4,3,2,1,0:T(8,128)S(1)}, f32[16,2,4,32,32]{4,3,2,1,0:T(8,128)}, u32[]{:S(2)}) %copy-start) | copy-done | bytes 524312
  48.8 0.0 copy-start.1
  48.8 1.4 %copy-done.1 = f32[16,2,3,32,32]{4,3,2,1,0:T(8,128)S(1)} copy-done((f32[16,2,3,32,32]{4,3,2,1,0:T(8,128)S(1)}, f32[16,2,3,32,32]{4,3,2,1,0:T(8,128)}, u32[]{:S(2)}) %copy-start.1) | copy-done | bytes 393240
  50.2 3.2 %shard_map.129.operator_ref = bf16[16,128,256]{2,1,0:T(8,128)(2,1)S(1)} custom-call(s32[16,8]{1,0:T(8,128)S(1)} %copy.17.columns_ref, f32[16,4,2,32,32]{4,3,2,1,0:T(8,128)S(1)} %reshape.27.blocks_ref, f32[16,2,4,32,32]{4,3,2,1,0:T(8,128)S(1)} %copy-done, f32[16,2,3,32,32]{4,3,2,1,0:T(8,128)S(1)} %copy-done.1), custom_call_target="tpu_custom_call" | custom-call | flops 276824064 | bytes 1442304 | tf_op jit(solution)/shard_map/pallas_call | solution.py:248
  53.4 0.0 copy-start.2
  53.4 0.0 copy-start.3
  53.4 4.9 %all-to-all-done.1 = f32[32,32,128]{2,1,0:T(8,128)} async-done(((f32[32,32,128]{2,1,0:T(8,128)}), f32[32,32,128]{2,1,0:T(8,128)}, u32[]{:S(2)}, u32[]{:S(2)}) %all-to-all-start.1) | async-done | bytes 524320 | tf_op jit(solution)/shard_map/all_to_all | solution.py:260
  58.3 2.3 %shard_map.130 = f32[1024,128]{1,0:T(8,128)S(1)} custom-call(f32[1024,128]{1,0:T(8,128)} %bitcast.1.in_ref, bf16[16,128,256]{2,1,0:T(8,128)(2,1)S(1)} %shard_map.129.operator_ref), custom_call_target="tpu_custom_call" | custom-call | flops 201326592 | bytes 1572864 | tf_op jit(solution)/shard_map/pallas_call | solution.py:248
  60.6 24.9 %all_to_all.21.in_ref = f32[32,32,128]{2,1,0:T(8,128)S(1)} all-to-all(f32[32,32,128]{2,1,0:T(8,128)S(1)} %bitcast.9), channel_id=1, replica_groups=mesh['gx'=16,'gy'=32] {'gy'}, dimensions={0} | all-to-all | bytes 1048576 | tf_op jit(solution)/shard_map/all_to_all | solution.py:260
  85.4 0.0 copy-done.2
  85.4 0.0 copy-done.3
  85.4 0.0 copy-start.6
  85.5 0.0 copy-start.7
  85.5 0.8 shard_map.131
  86.3 23.5 %all_to_all.22.in_ref = f32[16,64,128]{2,1,0:T(8,128)S(1)} all-to-all(f32[16,64,128]{2,1,0:T(8,128)S(1)} %bitcast.8), channel_id=1, replica_groups=mesh['gx'=16,'gy'=32] {'gx'}, dimensions={0} | all-to-all | bytes 1048576 | tf_op jit(solution)/shard_map/all_to_all | solution.py:260
  109.8 0.0 copy-done.6
  109.8 0.0 copy-done.7
  109.8 1.5 %shard_map.132 = f32[4,64,512]{2,1,0:T(8,128)} custom-call(f32[16,64,128]{2,1,0:T(8,128)S(1)} %all_to_all.22.in_ref, bf16[2,256,256]{2,1,0:T(8,128)(2,1)S(1)} %copy-done.6, bf16[2,256,256]{2,1,0:T(8,128)(2,1)S(1)} %copy-done.7), custom_call_target="tpu_custom_call" | custom-call | flops 201326592 | bytes 1048576 | tf_op jit(solution)/shard_map/pallas_call | solution.py:248
Async XLA Ops:
  0.0 23.4 %copy-start.4 = (bf16[4,256,512]{2,1,0:T(8,128)(2,1)S(1)}, bf16[4,256,512]{2,1,0:T(8,128)(2,1)}, u32[]{:S(2)}) copy-start(bf16[4,256,512]{2,1,0:T(8,128)(2,1)} %constant.18.clone.high_ref) | copy-start | bytes 3145732
  0.0 23.4 %copy-start.5 = (bf16[4,256,512]{2,1,0:T(8,128)(2,1)S(1)}, bf16[4,256,512]{2,1,0:T(8,128)(2,1)}, u32[]{:S(2)}) copy-start(bf16[4,256,512]{2,1,0:T(8,128)(2,1)} %constant.19.clone.low_ref) | copy-start | bytes 3145732
  23.4 18.6 %copy-start.10 = (f32[1,16,2,3,1024]{4,2,3,1,0:T(2,128)S(1)}, f32[1,16,2,3,1024]{4,2,3,1,0:T(2,128)}, u32[]{:S(2)}) copy-start(f32[1,16,2,3,1024]{4,2,3,1,0:T(2,128)} %param.17) | copy-start | bytes 1179652
  25.0 33.3 %all-to-all-start.1 = ((f32[32,32,128]{2,1,0:T(8,128)}), f32[32,32,128]{2,1,0:T(8,128)}, u32[]{:S(2)}, u32[]{:S(2)}) async-start(f32[32,32,128]{2,1,0:T(8,128)} %shard_map.128), calls=%async_computation.1 | async-start | bytes 1048576 | tf_op jit(solution)/shard_map/all_to_all | solution.py:260
  42.1 2.1 %copy-start.8 = (f32[1,16,4,2,1024]{4,3,2,1,0:T(2,128)S(1)}, f32[1,16,4,2,1024]{4,3,2,1,0:T(2,128)}, u32[]{:S(2)}) copy-start(f32[1,16,4,2,1024]{4,3,2,1,0:T(2,128)} %param.14) | copy-start | bytes 1572868
  42.8 2.2 %copy-start.9 = (f32[1,16,2,4,1024]{4,3,2,1,0:T(4,128)S(1)}, f32[1,16,2,4,1024]{4,3,2,1,0:T(4,128)}, u32[]{:S(2)}) copy-start(f32[1,16,2,4,1024]{4,3,2,1,0:T(4,128)} %param.16) | copy-start | bytes 1572868
  44.2 2.9 %copy-start.11 = (s32[1,16,4,2]{1,3,2,0:T(2,128)S(1)}, s32[1,16,4,2]{1,3,2,0:T(2,128)}, u32[]{:S(2)}) copy-start(s32[1,16,4,2]{1,3,2,0:T(2,128)} %param.15) | copy-start | bytes 1540
  47.2 1.6 %copy-start = (f32[16,2,4,32,32]{4,3,2,1,0:T(8,128)S(1)}, f32[16,2,4,32,32]{4,3,2,1,0:T(8,128)}, u32[]{:S(2)}) copy-start(f32[16,2,4,32,32]{4,3,2,1,0:T(8,128)} %reshape.28.diag_ref) | copy-start | bytes 1572868
  48.8 1.4 %copy-start.1 = (f32[16,2,3,32,32]{4,3,2,1,0:T(8,128)S(1)}, f32[16,2,3,32,32]{4,3,2,1,0:T(8,128)}, u32[]{:S(2)}) copy-start(f32[16,2,3,32,32]{4,3,2,1,0:T(8,128)} %copy.18.off_ref) | copy-start | bytes 1179652
  53.4 32.1 %copy-start.2 = (bf16[4,256,512]{2,1,0:T(8,128)(2,1)S(1)}, bf16[4,256,512]{2,1,0:T(8,128)(2,1)}, u32[]{:S(2)}) copy-start(bf16[4,256,512]{2,1,0:T(8,128)(2,1)} %constant.20.clone.high_ref) | copy-start | bytes 3145732
  53.4 32.1 %copy-start.3 = (bf16[4,256,512]{2,1,0:T(8,128)(2,1)S(1)}, bf16[4,256,512]{2,1,0:T(8,128)(2,1)}, u32[]{:S(2)}) copy-start(bf16[4,256,512]{2,1,0:T(8,128)(2,1)} %constant.21.clone.low_ref) | copy-start | bytes 3145732
  85.4 24.3 %copy-start.6 = (bf16[2,256,256]{2,1,0:T(8,128)(2,1)S(1)}, bf16[2,256,256]{2,1,0:T(8,128)(2,1)}, u32[]{:S(2)}) copy-start(bf16[2,256,256]{2,1,0:T(8,128)(2,1)} %constant.22.clone.high_ref) | copy-start | bytes 786436
  85.5 24.3 %copy-start.7 = (bf16[2,256,256]{2,1,0:T(8,128)(2,1)S(1)}, bf16[2,256,256]{2,1,0:T(8,128)(2,1)}, u32[]{:S(2)}) copy-start(bf16[2,256,256]{2,1,0:T(8,128)(2,1)} %constant.23.clone.low_ref) | copy-start | bytes 786436
where the time goes:
time: 113 us; the launch traced here: 111 us
  blocking collectives  68.8 us (61%)
  starting transfers between devices  17 us (15%)
  Pallas kernels  12.4 us (11%)
  local copies, waits for them, and re-layouts  8.07 us (7%)
  waiting for transfers between devices  4.88 us (4%)
    all_to_all x3, blocking collectives, exchange(): return lax.all_to_all(values, axis, split_axis=0, concat_axis=0, tiled=True)  68.8 us
    all_to_all x1, starting transfers between devices, exchange(): return lax.all_to_all(values, axis, split_axis=0, concat_axis=0, tiled=True)  17 us
    pallas_call x6, Pallas kernels, call(): pl.pallas_call(kernel, out_shape=jax.ShapeDtypeStruct(shape, dtype), in_s...  12.4 us
    all_to_all x1, waiting for transfers between devices, exchange(): return lax.all_to_all(values, axis, split_axis=0, concat_axis=0, tiled=True)  4.88 us
    unnamed x24, local copies, waits for them, and re-layouts  3.05 us
  transfers between devices with their start and end apart: 1, of which 1 were waited for; matrix products, arithmetic and copies ran while one was open for 5% of the time, Pallas kernels for 3%

commit v1 on v0

v1 whole, which is shorter than its diff:
```python
import functools
import math

import jax
import jax.numpy as jnp
import ml_dtypes
import numpy as np
from jax import lax
from jax.experimental import pallas as pl
from jax.experimental.pallas import tpu as pltpu
from jax.sharding import PartitionSpec as P

NX = 512
NY = 1024
QUARTER = NY // 4
HALF = NX // 2
LANES = 128
SPAN = 16
BLOCK = 32
PART = SPAN // 2
VMEM_LIMIT = 24 * 1024 * 1024

f32 = jnp.float32
bf16 = jnp.bfloat16


def split_table(table):
    high = table.astype(ml_dtypes.bfloat16)
    low = (table - high.astype(np.float64)).astype(ml_dtypes.bfloat16)
    return high, low


def x_tables():
    parity = np.arange(2).reshape(2, 1, 1)
    x = np.arange(HALF).reshape(1, HALF, 1)
    k = 2 * np.arange(HALF // 2).reshape(1, 1, HALF // 2) + parity
    angle = (x * k % NX) * (2.0 * math.pi / NX)
    shape = (2, HALF, HALF // SPAN, PART)
    cosine = np.cos(angle).reshape(shape) / math.sqrt(NX)
    sine = np.sin(angle).reshape(shape) / math.sqrt(NX)
    forward = np.stack([cosine, -sine], axis=3)
    weight = np.where(k == 0, 1.0, 2.0).reshape(2, 1, HALF // SPAN, 1, PART)
    backward = (forward * weight).reshape(2, HALF, HALF).transpose(0, 2, 1)
    return split_table(forward.reshape(2, HALF, HALF)), split_table(backward)


def y_tables():
    residue = np.arange(4).reshape(4, 1, 1)
    row = np.arange(QUARTER).reshape(1, QUARTER, 1)
    j = np.arange(QUARTER).reshape(1, 1, QUARTER)
    angle = (row * (residue + 4 * j) % NY) * (2.0 * math.pi / NY)
    cosine = np.cos(angle) / math.sqrt(NY)
    sine = np.sin(angle) / math.sqrt(NY)
    forward = np.concatenate([cosine, sine], axis=2)
    backward = np.concatenate([cosine, -sine], axis=2)
    return split_table(forward), split_table(backward)


def slab_order(count):
    levels = count // 4
    return [
        (high * levels + z) * 2 + core
        for core in (1, 0)
        for high in (1, 0)
        for z in range(levels - 1, -1, -1)
    ]


def line_order(count):
    side = math.isqrt(count)
    along_x = [*range(0, side, 2), *range(1, side, 2)]
    along_y = [0, side - 1, *range(1, side - 1)]
    return [side * y + x for x in along_x for y in along_y]


def order_tables(order):
    count = len(order)
    lane = np.arange(4 * count)
    index = 4 * np.array(order)[lane % count] + lane // count
    row = np.arange(BLOCK).reshape(BLOCK, 1)
    place = np.tile(index % BLOCK == row, (2, 1)).astype(ml_dtypes.bfloat16)
    owner = np.broadcast_to(index // BLOCK, (BLOCK, 4 * count)).astype(np.int32)
    pick = (index.reshape(-1, 1) == lane).astype(ml_dtypes.bfloat16)
    return place, owner, pick


def split(values):
    high = values.astype(bf16)
    low = (values - high.astype(f32)).astype(bf16)
    return high, low


def mul(left, right):
    return jnp.dot(left, right, preferred_element_type=f32)


def lane_index(shape):
    return lax.broadcasted_iota(jnp.int32, shape, len(shape) - 1)


def swap_groups(parts):
    parts = list(parts)
    lane = lane_index(parts[0].shape)
    distance, reach = len(parts) // 2, LANES // 2
    while distance:
        first = (lane & reach) == 0
        for i in range(len(parts)):
            if not i & distance:
                a, b = parts[i], parts[i + distance]
                parts[i] = jnp.where(first, a, pltpu.roll(b, reach, 1))
                parts[i + distance] = jnp.where(first, pltpu.roll(a, LANES - reach, 1), b)
        distance, reach = distance // 2, reach // 2
    return parts


def turned(values):
    real = (lane_index(values.shape) & PART) == 0
    return jnp.where(real, pltpu.roll(values, LANES - PART, 1), -pltpu.roll(values, PART, 1))


def x_forward_kernel(order, grid_hbm, high_hbm, low_hbm, out_ref, grid_ref, high_ref, low_ref, sems):
    depth, lines, length = grid_ref.shape
    pairs = [(high_hbm, high_ref), (low_hbm, low_ref)]
    pairs += [(grid_hbm.at[z], grid_ref.at[z]) for z in range(depth)]
    copies = [
        pltpu.make_async_copy(source, target, sems.at[i])
        for i, (source, target) in enumerate(pairs)
    ]
    for copy in copies:
        copy.start()
    for copy in copies:
        copy.wait()
    near = grid_ref[:, :, :HALF].reshape(depth * lines, HALF)
    far = grid_ref[:, :, HALF:].reshape(depth * lines, HALF)
    sums = []
    for p, values in enumerate((near + far, near - far)):
        high, low = split(values)
        wide = mul(jnp.concatenate([high, low], axis=0), high_ref[p])
        sums.append(wide[: depth * lines] + (wide[depth * lines :] + mul(high, low_ref[p])))
    for a in range(HALF // LANES):
        columns = slice(a * LANES, (a + 1) * LANES)
        parts = [
            sums[p][z * lines : (z + 1) * lines, columns] for z in range(depth) for p in range(2)
        ]
        for b, part in enumerate(swap_groups(parts)):
            out_ref[order.index(8 * a + b)] = part


def x_backward_kernel(order, in_ref, high_ref, low_ref, out_hbm, out_ref, sems):
    depth, lines, length = out_ref.shape
    columns = [
        swap_groups([in_ref[order.index(8 * a + b)] for b in range(8)])
        for a in range(HALF // LANES)
    ]
    step = 2
    copies = []
    for z in range(0, depth, step):
        levels = range(z, z + step)
        results = []
        for p in range(2):
            rows = [
                jnp.concatenate([column[2 * level + p] for column in columns], axis=1)
                for level in levels
            ]
            high, low = split(jnp.concatenate(rows, axis=0))
            wide = mul(jnp.concatenate([high, low], axis=0), high_ref[p])
            count = step * lines
            results.append(wide[:count] + (wide[count:] + mul(high, low_ref[p])))
        near, far = results
        out_ref[z : z + step, :, :HALF] = (near + far).reshape(step, lines, HALF)
        out_ref[z : z + step, :, HALF:] = (near - far).reshape(step, lines, HALF)
        for level in levels:
            copy = pltpu.make_async_copy(out_ref.at[level], out_hbm.at[level], sems.at[level])
            copy.start()
            copies.append(copy)
    for copy in copies:
        copy.wait()


def quarter_product(values, high_table, low_table):
    both = jnp.concatenate([values, turned(values)], axis=0)
    high, low = split(both)
    wide = mul(high_table, jnp.concatenate([high, low], axis=1))
    return wide[:, :LANES] + (wide[:, LANES:] + mul(low_table, high))


def load_blocks(ref, order, r):
    block = ref.shape[0] // len(order)
    parts = [
        ref[pl.ds(block * order.index(i) + r, block // 4, stride=4), :] for i in range(len(order))
    ]
    return jnp.concatenate(parts, axis=0)


def store_blocks(ref, order, quarters):
    block = ref.shape[0] // len(order)
    for place, i in enumerate(order):
        start = block * i % QUARTER
        part = quarters[block * i // QUARTER][start : start + block]
        ref[block * place : block * place + block, :] = part


def y_kernel(sign, source, target, in_ref, high_ref, low_ref, out_ref):
    products = [
        quarter_product(load_blocks(in_ref, source, r), high_ref[r], low_ref[r])
        for r in range(4)
    ]
    a, b, c, d = products
    even_sum, even_difference = a + c, a - c
    odd_sum, odd_difference = b + d, sign * turned(b - d)
    quarters = (
        even_sum + odd_sum,
        even_difference + odd_difference,
        even_sum - odd_sum,
        even_difference - odd_difference,
    )
    store_blocks(out_ref, target, quarters)


def spread_left(matrix):
    rest = matrix - matrix.astype(bf16).astype(f32)
    return jnp.concatenate([matrix, rest, matrix], axis=1).astype(bf16)


def three(matrix, right):
    high, low = split(right)
    return mul(spread_left(matrix), jnp.concatenate([high, high, low], axis=0))


def operator_kernel(
    columns_ref, blocks_ref, diag_ref, off_ref, place_ref, owner_ref, pick_ref, out_ref, hold_ref
):
    groups = blocks_ref.shape[0]
    place = place_ref[...]
    owner = owner_ref[...]

    def rows(i):
        return slice(BLOCK * i, BLOCK * i + BLOCK)

    for i in range(4):
        for g in range(groups):
            matrix = blocks_ref[g, i].reshape(2 * BLOCK, BLOCK)
            rest = matrix - matrix.astype(bf16).astype(f32)
            spread = mul(jnp.concatenate([matrix, rest], axis=1).astype(bf16), place)
            hold_ref[g, rows(i), :] = jnp.where(
                owner == columns_ref[g, 2 * i], spread[:BLOCK], 0.0
            ) + jnp.where(owner == columns_ref[g, 2 * i + 1], spread[BLOCK:], 0.0)
    for half, order in ((0, (0, 1, 2, 3)), (1, (3, 2, 1, 0))):
        for step, i in enumerate(order):
            if step:
                last = order[step - 1]
                coupled = min(i, last)
                for g in range(groups):
                    hold_ref[g, rows(i), :] -= three(
                        off_ref[g, half, coupled], hold_ref[g, rows(last), :]
                    )
            for g in range(groups):
                hold_ref[g, rows(i), :] = three(diag_ref[g, half, i], hold_ref[g, rows(i), :])
    pick = pick_ref[...]
    for g in range(groups):
        high, low = split(hold_ref[g])
        ordered = mul(pick, jnp.concatenate([high, low], axis=1))
        out_ref[g] = ordered.astype(bf16)


def apply_kernel(in_ref, operator_ref, out_ref):
    slabs = in_ref.shape[0] // 32
    first = lane_index((LANES, LANES)) < 64
    wide = []
    for r in range(8):
        parts = [in_ref[pl.ds(4 * r + i, slabs, stride=32), :] for i in range(4)]
        high, low = split(jnp.concatenate(swap_groups(parts), axis=0))
        upper = jnp.concatenate([high, low], axis=1)
        lower = jnp.concatenate([high, jnp.zeros_like(low)], axis=1)
        wide.append(jnp.concatenate([upper, lower], axis=0))
    solved = []
    for r in range(8):
        both = mul(operator_ref[2 * r : 2 * r + 2].reshape(2 * LANES, 2 * LANES), wide[r])
        both = both[:, :LANES] + both[:, LANES:]
        solved.append(jnp.where(first, both[:LANES], both[LANES:]))
    for r in range(8):
        parts = swap_groups([solved[r][32 * level : 32 * level + 32] for level in range(4)])
        for i in range(4):
            out_ref[pl.ds(4 * r + i, slabs, stride=32), :] = parts[i]


def call(kernel, shape, *operands, dtype=f32, spaces=None, out=None, scratch=(), flops=0):
    spaces = spaces or [None] * len(operands)
    read = sum(math.prod(o.shape) * o.dtype.itemsize for o in operands)
    operands = [
        operand if space in (None, pltpu.SMEM) else pltpu.with_memory_space_constraint(operand, space)
        for space, operand in zip(spaces, operands)
    ]
    return pl.pallas_call(
        kernel,
        out_shape=jax.ShapeDtypeStruct(shape, dtype),
        in_specs=[pl.BlockSpec(memory_space=space or pltpu.VMEM) for space in spaces],
        out_specs=pl.BlockSpec(memory_space=out or pltpu.VMEM),
        scratch_shapes=scratch,
        cost_estimate=pl.CostEstimate(flops=flops, bytes_accessed=read, transcendentals=0),
        compiler_params=pltpu.CompilerParams(vmem_limit_bytes=VMEM_LIMIT),
    )(*operands)


def exchange(values, axis, order=None):
    members = None if order is None else [order]
    return lax.all_to_all(
        values, axis, split_axis=0, concat_axis=0, axis_index_groups=members, tiled=True
    )


def body(grid_field, operator_blocks, op_columns, diag_inverse, off_blocks):
    depth, lines, length = grid_field.shape
    groups = operator_blocks.shape[1]
    forward_x, backward_x = x_tables()
    forward_y, backward_y = y_tables()
    order = slab_order(32)
    line = line_order(16)
    square = (BLOCK, BLOCK)
    operator = call(
        operator_kernel,
        (groups, LANES, 2 * LANES),
        op_columns.reshape(groups, 8),
        operator_blocks.reshape((groups, 4, 2) + square),
        diag_inverse.reshape((groups, 2, 4) + square),
        off_blocks.reshape((groups, 2, 3) + square),
        *order_tables(order),
        dtype=bf16,
        spaces=[pltpu.SMEM] + [None] * 6,
        scratch=[pltpu.VMEM((groups, LANES, LANES), f32)],
        flops=2 * 3 * groups * 22 * BLOCK * BLOCK * LANES,
    )
    x_flops = 2 * 3 * depth * lines * length * HALF
    y_flops = 2 * 3 * 4 * QUARTER * 2 * QUARTER * LANES
    values = call(
        functools.partial(x_forward_kernel, line),
        (16, lines, LANES),
        grid_field,
        *forward_x,
        spaces=[pltpu.HBM] * 3,
        scratch=[
            pltpu.VMEM(grid_field.shape, f32),
            pltpu.VMEM((2, HALF, HALF), bf16),
            pltpu.VMEM((2, HALF, HALF), bf16),
            pltpu.SemaphoreType.DMA((2 + depth,)),
        ],
        flops=x_flops,
    )
    values = exchange(values, "gx", line).reshape(NY, LANES)
    values = call(
        functools.partial(y_kernel, 1.0, line, order), (NY, LANES), values, *forward_y, flops=y_flops
    )
    values = exchange(values.reshape(32, 32, LANES), "gy", order).reshape(NY, LANES)
    values = call(
        apply_kernel,
        (NY, LANES),
        values,
        operator,
        flops=2 * 3 * groups * LANES * LANES * LANES,
    )
    values = exchange(values.reshape(32, 32, LANES), "gy", order).reshape(NY, LANES)
    values = call(
        functools.partial(y_kernel, -1.0, order, line), (NY, LANES), values, *backward_y, flops=y_flops
    )
    values = exchange(values.reshape(16, lines, LANES), "gx", line)
    return call(
        functools.partial(x_backward_kernel, line),
        (depth, lines, length),
        values,
        *backward_x,
        out=pl.ANY,
        scratch=[pltpu.VMEM((depth, lines, length), f32), pltpu.SemaphoreType.DMA((depth,))],
        flops=x_flops,
    )


def solution(mesh):
    placed = (
        P("gy", "gx", None),
        P("gx", "gy", None, None, None),
        P("gx", "gy", None, None),
        P("gx", "gy", None, None, None),
        P("gx", "gy", None, None, None),
    )
    return jax.shard_map(
        body, mesh=mesh, in_specs=placed, out_specs=P("gy", "gx", None), check_vma=False
    )
```

time: 113 us -> 106 us (0.938)
  blocking collectives: 68.8 us -> 59.8 us
  starting transfers between devices: 17 us -> 21 us
  waiting for transfers between devices: 4.88 us -> 3.52 us
    all_to_all x3, blocking collectives: 68.8 us -> 59.8 us  [exchange(): lax.all_to_all(values, axis, split_axis=0, concat_axis=0, axis_index_grou...]
    all_to_all x1, starting transfers between devices: 17 us -> 21 us  [exchange(): lax.all_to_all(values, axis, split_axis=0, concat_axis=0, axis_index_grou...]
    all_to_all x1, waiting for transfers between devices: 4.88 us -> 3.52 us  [exchange(): lax.all_to_all(values, axis, split_axis=0, concat_axis=0, axis_index_grou...]
    unnamed x24 -> x30, local copies, waits for them, and re-layouts: 3.05 us -> 3.19 us
where the time goes in v1:
time: 106 us; the launch traced here: 104 us
  blocking collectives  59.8 us (56%)
  starting transfers between devices  21 us (20%)
  Pallas kernels  11.8 us (11%)
  local copies, waits for them, and re-layouts  8.2 us (8%)
  waiting for transfers between devices  3.52 us (3%)
    all_to_all x3, blocking collectives, exchange(): lax.all_to_all(values, axis, split_axis=0, concat_axis=0, axis_index_grou...  59.8 us
    all_to_all x1, starting transfers between devices, exchange(): lax.all_to_all(values, axis, split_axis=0, concat_axis=0, axis_index_grou...  21 us
    pallas_call x6, Pallas kernels, call(): pl.pallas_call(kernel, out_shape=jax.ShapeDtypeStruct(shape, dtype), in_s...  11.8 us
    all_to_all x1, waiting for transfers between devices, exchange(): lax.all_to_all(values, axis, split_axis=0, concat_axis=0, axis_index_grou...  3.52 us
    unnamed x30, local copies, waits for them, and re-layouts  3.19 us
  transfers between devices with their start and end apart: 1, of which 1 were waited for; matrix products, arithmetic and copies ran while one was open for 5% of the time, Pallas kernels for 3%

profile of v1, /device:TPU:1, one launch (start us, length us, event | category | flops | bytes accessed | tf_op | source)
XLA Modules:
  0.0 104.4 jit_solution(16646309980972504748)
XLA Ops:
  0.0 0.0 copy-start.4
  0.0 0.0 copy-start.5
  0.0 2.2 %shard_map.154 = f32[16,64,128]{2,1,0:T(8,128)S(1)} custom-call(f32[4,64,512]{2,1,0:T(8,128)} %grid_hbm.1, bf16[2,256,256]{2,1,0:T(8,128)(2,1)} %constant.25.clone.high_hbm, bf16[2,256,256]{2,1,0:T(8,128)(2,1)} %constant.26.clone.low_hbm), custom_call_target="tpu_custom_call" | custom-call | flops 201326592 | bytes 1048576 | tf_op jit(solution)/shard_map/pallas_call | solution.py:294
  2.2 18.8 %all_to_all.20 = f32[16,64,128]{2,1,0:T(8,128)S(1)} all-to-all(f32[16,64,128]{2,1,0:T(8,128)S(1)} %shard_map.154), channel_id=1, replica_groups={{0,384,128,256,64,448,192,320,32,416,160,288,96,480,224,352},{1,385,129..., dimensions={0} | all-to-all | bytes 1048576 | tf_op jit(solution)/shard_map/all_to_all | solution.py:307
  20.9 0.0 copy-done.4
  20.9 0.0 copy-done.5
  20.9 0.0 copy-start.13
  20.9 1.6 %shard_map.155 = f32[1024,128]{1,0:T(8,128)} custom-call(f32[1024,128]{1,0:T(8,128)S(1)} %bitcast.9, bf16[4,256,512]{2,1,0:T(8,128)(2,1)S(1)} %copy-done.4, bf16[4,256,512]{2,1,0:T(8,128)(2,1)S(1)} %copy-done.5), custom_call_target="tpu_custom_call" | custom-call | flops 402653184 | bytes 2621440 | tf_op jit(solution)/shard_map/pallas_call | solution.py:294
  22.6 21.0 %all-to-all-start.1 = ((f32[32,32,128]{2,1,0:T(8,128)}), f32[32,32,128]{2,1,0:T(8,128)}, u32[]{:S(2)}, u32[]{:S(2)}) async-start(f32[32,32,128]{2,1,0:T(8,128)} %bitcast.1), calls=%async_computation.1 | async-start | bytes 1048576 | tf_op jit(solution)/shard_map/all_to_all | solution.py:307
  43.6 0.0 copy-done.13
  43.6 0.0 copy-start.11
  43.6 0.7 reshape.40
  44.3 1.3 %copy.21.off_ref = f32[16,2,3,32,32]{4,3,2,1,0:T(8,128)} copy(f32[16,2,3,32,32]{4,3,1,2,0:T(8,128)S(1)} %reshape.40) | data formatting | bytes 786432 | tf_op jit(solution)/shard_map/reshape | solution.py:326
  45.6 0.0 copy-done.11
  45.6 0.0 copy-start.12
  45.6 0.0 copy-start.14
  45.6 0.0 copy-start.8
  45.6 0.0 copy-start.9
  45.6 0.0 copy-start.10
  45.7 0.9 reshape.34.blocks_ref
  46.5 0.1 copy-done.12
  46.7 2.0 %reshape.35.diag_ref = f32[16,2,4,32,32]{4,3,2,1,0:T(8,128)} reshape(f32[1,16,2,4,1024]{4,3,2,1,0:T(4,128)S(1)} %copy-done.12) | data formatting | bytes 1048576 | tf_op jit(solution)/shard_map/reshape | solution.py:325
  48.7 0.0 copy-done.14
  48.7 0.1 copy.20.columns_ref
  48.8 0.0 copy-done.8
  48.8 0.0 copy-done.9
  48.8 0.0 copy-done.10
  48.8 0.0 copy-start
  48.8 1.6 %copy-done = f32[16,2,4,32,32]{4,3,2,1,0:T(8,128)S(1)} copy-done((f32[16,2,4,32,32]{4,3,2,1,0:T(8,128)S(1)}, f32[16,2,4,32,32]{4,3,2,1,0:T(8,128)}, u32[]{:S(2)}) %copy-start) | copy-done | bytes 524312
  50.4 0.0 copy-start.1
  50.4 1.4 %copy-done.1 = f32[16,2,3,32,32]{4,3,2,1,0:T(8,128)S(1)} copy-done((f32[16,2,3,32,32]{4,3,2,1,0:T(8,128)S(1)}, f32[16,2,3,32,32]{4,3,2,1,0:T(8,128)}, u32[]{:S(2)}) %copy-start.1) | copy-done | bytes 393240
  51.8 3.5 %shard_map.156.operator_ref = bf16[16,128,256]{2,1,0:T(8,128)(2,1)S(1)} custom-call(s32[16,8]{1,0:T(8,128)S(1)} %copy.20.columns_ref, f32[16,4,2,32,32]{4,3,2,1,0:T(8,128)S(1)} %reshape.34.blocks_ref, f32[16,2,4,32,32]{4,3,2,1,0:T(8,128)S(1)} %copy-done, f32[16,2,3,32,32]{4,3,2,1,0:T(8,128)S(1)} %copy-done.1, bf16[64,128]{1,0:T(8,128)(2,1)S(1)} %copy-done.9, ...), custom_call_target="tpu_custom_call" | custom-call | flops 276824064 | bytes 1507840 | tf_op jit(solution)/shard_map/pallas_call | solution.py:294
  55.3 0.0 copy-start.2
  55.3 0.0 copy-start.3
  55.3 3.5 %all-to-all-done.1 = f32[32,32,128]{2,1,0:T(8,128)} async-done(((f32[32,32,128]{2,1,0:T(8,128)}), f32[32,32,128]{2,1,0:T(8,128)}, u32[]{:S(2)}, u32[]{:S(2)}) %all-to-all-start.1) | async-done | bytes 524320 | tf_op jit(solution)/shard_map/all_to_all | solution.py:307
  58.9 2.2 %shard_map.157 = f32[1024,128]{1,0:T(8,128)S(1)} custom-call(f32[1024,128]{1,0:T(8,128)} %bitcast.2.in_ref, bf16[16,128,256]{2,1,0:T(8,128)(2,1)S(1)} %shard_map.156.operator_ref), custom_call_target="tpu_custom_call" | custom-call | flops 201326592 | bytes 1572864 | tf_op jit(solution)/shard_map/pallas_call | solution.py:294
  61.1 24.6 %all_to_all.21 = f32[32,32,128]{2,1,0:T(8,128)S(1)} all-to-all(f32[32,32,128]{2,1,0:T(8,128)S(1)} %bitcast.12), channel_id=1, replica_groups={{31,29,27,25,23,21,19,17,15,13,11,9,7,5,3,1,30,28,26,24,22,20,18,16,14,..., dimensions={0} | all-to-all | bytes 1048576 | tf_op jit(solution)/shard_map/all_to_all | solution.py:307
  85.7 0.0 copy-done.2
  85.7 0.0 copy-done.3
  85.7 0.0 copy-start.6
  85.7 0.0 copy-start.7
  85.7 0.8 shard_map.158
  86.6 16.4 %all_to_all.22.in_ref = f32[16,64,128]{2,1,0:T(8,128)S(1)} all-to-all(f32[16,64,128]{2,1,0:T(8,128)S(1)} %bitcast.11), channel_id=1, replica_groups={{0,384,128,256,64,448,192,320,32,416,160,288,96,480,224,352},{1,385,129..., dimensions={0} | all-to-all | bytes 1048576 | tf_op jit(solution)/shard_map/all_to_all | solution.py:307
  103.0 0.0 copy-done.6
  103.0 0.0 copy-done.7
  103.0 1.4 %shard_map.159 = f32[4,64,512]{2,1,0:T(8,128)} custom-call(f32[16,64,128]{2,1,0:T(8,128)S(1)} %all_to_all.22.in_ref, bf16[2,256,256]{2,1,0:T(8,128)(2,1)S(1)} %copy-done.6, bf16[2,256,256]{2,1,0:T(8,128)(2,1)S(1)} %copy-done.7), custom_call_target="tpu_custom_call" | custom-call | flops 201326592 | bytes 1048576 | tf_op jit(solution)/shard_map/pallas_call | solution.py:294
Async XLA Ops:
  0.0 20.9 %copy-start.4 = (bf16[4,256,512]{2,1,0:T(8,128)(2,1)S(1)}, bf16[4,256,512]{2,1,0:T(8,128)(2,1)}, u32[]{:S(2)}) copy-start(bf16[4,256,512]{2,1,0:T(8,128)(2,1)} %constant.27.clone.high_ref) | copy-start | bytes 3145732
  0.0 20.9 %copy-start.5 = (bf16[4,256,512]{2,1,0:T(8,128)(2,1)S(1)}, bf16[4,256,512]{2,1,0:T(8,128)(2,1)}, u32[]{:S(2)}) copy-start(bf16[4,256,512]{2,1,0:T(8,128)(2,1)} %constant.28.clone.low_ref) | copy-start | bytes 3145732
  20.9 22.6 %copy-start.13 = (f32[1,16,2,3,1024]{4,2,3,1,0:T(2,128)S(1)}, f32[1,16,2,3,1024]{4,2,3,1,0:T(2,128)}, u32[]{:S(2)}) copy-start(f32[1,16,2,3,1024]{4,2,3,1,0:T(2,128)} %param.20) | copy-start | bytes 1179652
  22.6 36.3 %all-to-all-start.1 = ((f32[32,32,128]{2,1,0:T(8,128)}), f32[32,32,128]{2,1,0:T(8,128)}, u32[]{:S(2)}, u32[]{:S(2)}) async-start(f32[32,32,128]{2,1,0:T(8,128)} %bitcast.1), calls=%async_computation.1 | async-start | bytes 1048576 | tf_op jit(solution)/shard_map/all_to_all | solution.py:307
  43.6 2.0 %copy-start.11 = (f32[1,16,4,2,1024]{4,3,2,1,0:T(2,128)S(1)}, f32[1,16,4,2,1024]{4,3,2,1,0:T(2,128)}, u32[]{:S(2)}) copy-start(f32[1,16,4,2,1024]{4,3,2,1,0:T(2,128)} %param.17) | copy-start | bytes 1572868
  45.6 1.0 copy-start.12
  45.6 3.1 %copy-start.14 = (s32[1,16,4,2]{1,3,2,0:T(2,128)S(1)}, s32[1,16,4,2]{1,3,2,0:T(2,128)}, u32[]{:S(2)}) copy-start(s32[1,16,4,2]{1,3,2,0:T(2,128)} %param.18) | copy-start | bytes 1540
  45.6 3.2 %copy-start.8 = (bf16[128,128]{1,0:T(8,128)(2,1)S(1)}, bf16[128,128]{1,0:T(8,128)(2,1)}, u32[]{:S(2)}) copy-start(bf16[128,128]{1,0:T(8,128)(2,1)} %constant.24.clone.pick_ref) | copy-start | bytes 98308
  45.6 3.2 %copy-start.9 = (bf16[64,128]{1,0:T(8,128)(2,1)S(1)}, bf16[64,128]{1,0:T(8,128)(2,1)}, u32[]{:S(2)}) copy-start(bf16[64,128]{1,0:T(8,128)(2,1)} %constant.22.clone.place_ref) | copy-start | bytes 49156
  45.6 3.2 %copy-start.10 = (s32[32,128]{1,0:T(8,128)S(1)}, s32[32,128]{1,0:T(8,128)}, u32[]{:S(2)}) copy-start(s32[32,128]{1,0:T(8,128)} %constant.23.clone.owner_ref) | copy-start | bytes 49156
  48.8 1.6 %copy-start = (f32[16,2,4,32,32]{4,3,2,1,0:T(8,128)S(1)}, f32[16,2,4,32,32]{4,3,2,1,0:T(8,128)}, u32[]{:S(2)}) copy-start(f32[16,2,4,32,32]{4,3,2,1,0:T(8,128)} %reshape.35.diag_ref) | copy-start | bytes 1572868
  50.4 1.4 %copy-start.1 = (f32[16,2,3,32,32]{4,3,2,1,0:T(8,128)S(1)}, f32[16,2,3,32,32]{4,3,2,1,0:T(8,128)}, u32[]{:S(2)}) copy-start(f32[16,2,3,32,32]{4,3,2,1,0:T(8,128)} %copy.21.off_ref) | copy-start | bytes 1179652
  55.3 30.4 %copy-start.2 = (bf16[4,256,512]{2,1,0:T(8,128)(2,1)S(1)}, bf16[4,256,512]{2,1,0:T(8,128)(2,1)}, u32[]{:S(2)}) copy-start(bf16[4,256,512]{2,1,0:T(8,128)(2,1)} %constant.29.clone.high_ref) | copy-start | bytes 3145732
  55.3 30.4 %copy-start.3 = (bf16[4,256,512]{2,1,0:T(8,128)(2,1)S(1)}, bf16[4,256,512]{2,1,0:T(8,128)(2,1)}, u32[]{:S(2)}) copy-start(bf16[4,256,512]{2,1,0:T(8,128)(2,1)} %constant.30.clone.low_ref) | copy-start | bytes 3145732
  85.7 17.3 %copy-start.6 = (bf16[2,256,256]{2,1,0:T(8,128)(2,1)S(1)}, bf16[2,256,256]{2,1,0:T(8,128)(2,1)}, u32[]{:S(2)}) copy-start(bf16[2,256,256]{2,1,0:T(8,128)(2,1)} %constant.31.clone.high_ref) | copy-start | bytes 786436
  85.7 17.3 %copy-start.7 = (bf16[2,256,256]{2,1,0:T(8,128)(2,1)S(1)}, bf16[2,256,256]{2,1,0:T(8,128)(2,1)}, u32[]{:S(2)}) copy-start(bf16[2,256,256]{2,1,0:T(8,128)(2,1)} %constant.32.clone.low_ref) | copy-start | bytes 786436

commit v2 on v1

--- a/solution.py
+++ b/solution.py
@@ -59,18 +59,15 @@
 def slab_order(count):
     levels = count // 4
     return [
-        (high * levels + z) * 2 + core
+        (high * levels + (levels - 2 - i) % levels) * 2 + core
+        for high in (1, 0)
         for core in (1, 0)
-        for high in (1, 0)
-        for z in range(levels - 1, -1, -1)
-    ]
-
-
-def line_order(count):
-    side = math.isqrt(count)
-    along_x = [*range(0, side, 2), *range(1, side, 2)]
-    along_y = [0, side - 1, *range(1, side - 1)]
-    return [side * y + x for x in along_x for y in along_y]
+        for i in range(levels)
+    ]
+
+
+def line_order():
+    return [4 * y + x for x in (1, 3, 2, 0) for y in (2, 1, 0, 3)]
 
 
 def order_tables(order):
@@ -120,23 +117,32 @@
 
 def x_forward_kernel(order, grid_hbm, high_hbm, low_hbm, out_ref, grid_ref, high_ref, low_ref, sems):
     depth, lines, length = grid_ref.shape
-    pairs = [(high_hbm, high_ref), (low_hbm, low_ref)]
-    pairs += [(grid_hbm.at[z], grid_ref.at[z]) for z in range(depth)]
+    levels = [(grid_hbm.at[z], grid_ref.at[z]) for z in range(depth)]
+    half = depth // 2
+    pairs = [(high_hbm, high_ref), *levels, (low_hbm, low_ref)]
     copies = [
         pltpu.make_async_copy(source, target, sems.at[i])
         for i, (source, target) in enumerate(pairs)
     ]
     for copy in copies:
         copy.start()
-    for copy in copies:
-        copy.wait()
-    near = grid_ref[:, :, :HALF].reshape(depth * lines, HALF)
-    far = grid_ref[:, :, HALF:].reshape(depth * lines, HALF)
-    sums = []
-    for p, values in enumerate((near + far, near - far)):
-        high, low = split(values)
-        wide = mul(jnp.concatenate([high, low], axis=0), high_ref[p])
-        sums.append(wide[: depth * lines] + (wide[depth * lines :] + mul(high, low_ref[p])))
+    rows = lines * half
+    sums = [[], []]
+    for part in range(2):
+        for copy in copies[1:][part * half : (part + 1) * half] if part else copies[: 1 + half]:
+            copy.wait()
+        window = slice(part * half, (part + 1) * half)
+        near = grid_ref[window, :, :HALF].reshape(rows, HALF)
+        far = grid_ref[window, :, HALF:].reshape(rows, HALF)
+        for p, values in enumerate((near + far, near - far)):
+            high, low = split(values)
+            wide = mul(jnp.concatenate([high, low], axis=0), high_ref[p])
+            sums[p].append((high, wide[:rows] + wide[rows:]))
+    copies[-1].wait()
+    sums = [
+        jnp.concatenate([total + mul(high, low_ref[p]) for high, total in sums[p]], axis=0)
+        for p in range(2)
+    ]
     for a in range(HALF // LANES):
         columns = slice(a * LANES, (a + 1) * LANES)
         parts = [
@@ -315,7 +321,7 @@
     forward_x, backward_x = x_tables()
     forward_y, backward_y = y_tables()
     order = slab_order(32)
-    line = line_order(16)
+    line = line_order()
     square = (BLOCK, BLOCK)
     operator = call(
         operator_kernel,

time: 106 us -> 103 us (0.972)
  starting transfers between devices: 21 us -> 19.3 us
    all_to_all x1, starting transfers between devices: 21 us -> 19.3 us  [exchange(): lax.all_to_all(values, axis, split_axis=0, concat_axis=0, axis_index_grou...]
where the time goes in v2:
time: 103 us; the launch traced here: 102 us
  blocking collectives  60.2 us (58%)
  starting transfers between devices  19.3 us (19%)
  Pallas kernels  11.8 us (11%)
  local copies, waits for them, and re-layouts  8.2 us (8%)
  waiting for transfers between devices  2.55 us (2%)
    all_to_all x3, blocking collectives, exchange(): lax.all_to_all(values, axis, split_axis=0, concat_axis=0, axis_index_grou...  60.2 us
    all_to_all x1, starting transfers between devices, exchange(): lax.all_to_all(values, axis, split_axis=0, concat_axis=0, axis_index_grou...  19.3 us
    pallas_call x6, Pallas kernels, call(): pl.pallas_call(kernel, out_shape=jax.ShapeDtypeStruct(shape, dtype), in_s...  11.8 us
    unnamed x30, local copies, waits for them, and re-layouts  3.19 us
    all_to_all x1, waiting for transfers between devices, exchange(): lax.all_to_all(values, axis, split_axis=0, concat_axis=0, axis_index_grou...  2.55 us
  transfers between devices with their start and end apart: 1, of which 1 were waited for; matrix products, arithmetic and copies ran while one was open for 5% of the time, Pallas kernels for 3%

profile of v2, /device:TPU:1, one launch (start us, length us, event | category | flops | bytes accessed | tf_op | source)
XLA Modules:
  0.0 102.2 jit_solution(7076854426965504232)
XLA Ops:
  0.0 0.0 copy-start.4
  0.0 0.0 copy-start.5
  0.0 2.1 %shard_map.154 = f32[16,64,128]{2,1,0:T(8,128)S(1)} custom-call(f32[4,64,512]{2,1,0:T(8,128)} %grid_hbm.1, bf16[2,256,256]{2,1,0:T(8,128)(2,1)} %constant.25.clone.high_hbm, bf16[2,256,256]{2,1,0:T(8,128)(2,1)} %constant.26.clone.low_hbm), custom_call_target="tpu_custom_call" | custom-call | flops 201326592 | bytes 1048576 | tf_op jit(solution)/shard_map/pallas_call | solution.py:300
  2.1 18.2 %all_to_all.20 = f32[16,64,128]{2,1,0:T(8,128)S(1)} all-to-all(f32[16,64,128]{2,1,0:T(8,128)S(1)} %shard_map.154), channel_id=1, replica_groups={{288,160,32,416,352,224,96,480,320,192,64,448,256,128,0,384},{289,161,3..., dimensions={0} | all-to-all | bytes 1048576 | tf_op jit(solution)/shard_map/all_to_all | solution.py:313
  20.3 0.0 copy-done.4
  20.4 0.0 copy-done.5
  20.4 0.0 copy-start.13
  20.4 1.6 %shard_map.155 = f32[1024,128]{1,0:T(8,128)} custom-call(f32[1024,128]{1,0:T(8,128)S(1)} %bitcast.9, bf16[4,256,512]{2,1,0:T(8,128)(2,1)S(1)} %copy-done.4, bf16[4,256,512]{2,1,0:T(8,128)(2,1)S(1)} %copy-done.5), custom_call_target="tpu_custom_call" | custom-call | flops 402653184 | bytes 2621440 | tf_op jit(solution)/shard_map/pallas_call | solution.py:300
  22.0 19.3 %all-to-all-start.1 = ((f32[32,32,128]{2,1,0:T(8,128)}), f32[32,32,128]{2,1,0:T(8,128)}, u32[]{:S(2)}, u32[]{:S(2)}) async-start(f32[32,32,128]{2,1,0:T(8,128)} %bitcast.1), calls=%async_computation.1 | async-start | bytes 1048576 | tf_op jit(solution)/shard_map/all_to_all | solution.py:313
  41.3 0.0 copy-done.13
  41.3 0.0 copy-start.11
  41.3 0.7 reshape.40
  42.0 1.3 %copy.21.off_ref = f32[16,2,3,32,32]{4,3,2,1,0:T(8,128)} copy(f32[16,2,3,32,32]{4,3,1,2,0:T(8,128)S(1)} %reshape.40) | data formatting | bytes 786432 | tf_op jit(solution)/shard_map/reshape | solution.py:332
  43.4 0.0 copy-done.11
  43.4 0.0 copy-start.12
  43.4 0.0 copy-start.14
  43.4 0.0 copy-start.8
  43.4 0.0 copy-start.9
  43.4 0.0 copy-start.10
  43.4 0.9 reshape.34.blocks_ref
  44.3 0.1 copy-done.12
  44.4 2.0 %reshape.35.diag_ref = f32[16,2,4,32,32]{4,3,2,1,0:T(8,128)} reshape(f32[1,16,2,4,1024]{4,3,2,1,0:T(4,128)S(1)} %copy-done.12) | data formatting | bytes 1048576 | tf_op jit(solution)/shard_map/reshape | solution.py:331
  46.5 0.0 copy-done.14
  46.5 0.1 copy.20.columns_ref
  46.5 0.0 copy-done.8
  46.5 0.0 copy-done.9
  46.5 0.0 copy-done.10
  46.6 0.0 copy-start
  46.6 1.6 %copy-done = f32[16,2,4,32,32]{4,3,2,1,0:T(8,128)S(1)} copy-done((f32[16,2,4,32,32]{4,3,2,1,0:T(8,128)S(1)}, f32[16,2,4,32,32]{4,3,2,1,0:T(8,128)}, u32[]{:S(2)}) %copy-start) | copy-done | bytes 524312
  48.1 0.0 copy-start.1
  48.1 1.4 %copy-done.1 = f32[16,2,3,32,32]{4,3,2,1,0:T(8,128)S(1)} copy-done((f32[16,2,3,32,32]{4,3,2,1,0:T(8,128)S(1)}, f32[16,2,3,32,32]{4,3,2,1,0:T(8,128)}, u32[]{:S(2)}) %copy-start.1) | copy-done | bytes 393240
  49.6 3.5 %shard_map.156.operator_ref = bf16[16,128,256]{2,1,0:T(8,128)(2,1)S(1)} custom-call(s32[16,8]{1,0:T(8,128)S(1)} %copy.20.columns_ref, f32[16,4,2,32,32]{4,3,2,1,0:T(8,128)S(1)} %reshape.34.blocks_ref, f32[16,2,4,32,32]{4,3,2,1,0:T(8,128)S(1)} %copy-done, f32[16,2,3,32,32]{4,3,2,1,0:T(8,128)S(1)} %copy-done.1, bf16[64,128]{1,0:T(8,128)(2,1)S(1)} %copy-done.9, ...), custom_call_target="tpu_custom_call" | custom-call | flops 276824064 | bytes 1507840 | tf_op jit(solution)/shard_map/pallas_call | solution.py:300
  53.1 0.0 copy-start.2
  53.1 0.0 copy-start.3
  53.1 2.5 %all-to-all-done.1 = f32[32,32,128]{2,1,0:T(8,128)} async-done(((f32[32,32,128]{2,1,0:T(8,128)}), f32[32,32,128]{2,1,0:T(8,128)}, u32[]{:S(2)}, u32[]{:S(2)}) %all-to-all-start.1) | async-done | bytes 524320 | tf_op jit(solution)/shard_map/all_to_all | solution.py:313
  55.7 2.2 %shard_map.157 = f32[1024,128]{1,0:T(8,128)S(1)} custom-call(f32[1024,128]{1,0:T(8,128)} %bitcast.2.in_ref, bf16[16,128,256]{2,1,0:T(8,128)(2,1)S(1)} %shard_map.156.operator_ref), custom_call_target="tpu_custom_call" | custom-call | flops 201326592 | bytes 1572864 | tf_op jit(solution)/shard_map/pallas_call | solution.py:300
  57.9 24.6 %all_to_all.21 = f32[32,32,128]{2,1,0:T(8,128)S(1)} all-to-all(f32[32,32,128]{2,1,0:T(8,128)S(1)} %bitcast.12), channel_id=1, replica_groups={{29,27,25,23,21,19,17,31,28,26,24,22,20,18,16,30,13,11,9,7,5,3,1,15,12,..., dimensions={0} | all-to-all | bytes 1048576 | tf_op jit(solution)/shard_map/all_to_all | solution.py:313
  82.5 0.0 copy-done.2
  82.5 0.0 copy-done.3
  82.5 0.0 copy-start.6
  82.5 0.0 copy-start.7
  82.5 0.8 shard_map.158
  83.4 17.4 %all_to_all.22.in_ref = f32[16,64,128]{2,1,0:T(8,128)S(1)} all-to-all(f32[16,64,128]{2,1,0:T(8,128)S(1)} %bitcast.11), channel_id=1, replica_groups={{288,160,32,416,352,224,96,480,320,192,64,448,256,128,0,384},{289,161,3..., dimensions={0} | all-to-all | bytes 1048576 | tf_op jit(solution)/shard_map/all_to_all | solution.py:313
  100.8 0.0 copy-done.6
  100.8 0.0 copy-done.7
  100.8 1.4 %shard_map.159 = f32[4,64,512]{2,1,0:T(8,128)} custom-call(f32[16,64,128]{2,1,0:T(8,128)S(1)} %all_to_all.22.in_ref, bf16[2,256,256]{2,1,0:T(8,128)(2,1)S(1)} %copy-done.6, bf16[2,256,256]{2,1,0:T(8,128)(2,1)S(1)} %copy-done.7), custom_call_target="tpu_custom_call" | custom-call | flops 201326592 | bytes 1048576 | tf_op jit(solution)/shard_map/pallas_call | solution.py:300
Async XLA Ops:
  0.0 20.3 %copy-start.4 = (bf16[4,256,512]{2,1,0:T(8,128)(2,1)S(1)}, bf16[4,256,512]{2,1,0:T(8,128)(2,1)}, u32[]{:S(2)}) copy-start(bf16[4,256,512]{2,1,0:T(8,128)(2,1)} %constant.27.clone.high_ref) | copy-start | bytes 3145732
  0.0 20.3 %copy-start.5 = (bf16[4,256,512]{2,1,0:T(8,128)(2,1)S(1)}, bf16[4,256,512]{2,1,0:T(8,128)(2,1)}, u32[]{:S(2)}) copy-start(bf16[4,256,512]{2,1,0:T(8,128)(2,1)} %constant.28.clone.low_ref) | copy-start | bytes 3145732
  20.4 21.0 %copy-start.13 = (f32[1,16,2,3,1024]{4,2,3,1,0:T(2,128)S(1)}, f32[1,16,2,3,1024]{4,2,3,1,0:T(2,128)}, u32[]{:S(2)}) copy-start(f32[1,16,2,3,1024]{4,2,3,1,0:T(2,128)} %param.20) | copy-start | bytes 1179652
  22.0 33.7 %all-to-all-start.1 = ((f32[32,32,128]{2,1,0:T(8,128)}), f32[32,32,128]{2,1,0:T(8,128)}, u32[]{:S(2)}, u32[]{:S(2)}) async-start(f32[32,32,128]{2,1,0:T(8,128)} %bitcast.1), calls=%async_computation.1 | async-start | bytes 1048576 | tf_op jit(solution)/shard_map/all_to_all | solution.py:313
  41.3 2.0 %copy-start.11 = (f32[1,16,4,2,1024]{4,3,2,1,0:T(2,128)S(1)}, f32[1,16,4,2,1024]{4,3,2,1,0:T(2,128)}, u32[]{:S(2)}) copy-start(f32[1,16,4,2,1024]{4,3,2,1,0:T(2,128)} %param.17) | copy-start | bytes 1572868
  43.4 1.0 %copy-start.12 = (f32[1,16,2,4,1024]{4,3,2,1,0:T(4,128)S(1)}, f32[1,16,2,4,1024]{4,3,2,1,0:T(4,128)}, u32[]{:S(2)}) copy-start(f32[1,16,2,4,1024]{4,3,2,1,0:T(4,128)} %param.19) | copy-start | bytes 1572868
  43.4 3.1 %copy-start.14 = (s32[1,16,4,2]{1,3,2,0:T(2,128)S(1)}, s32[1,16,4,2]{1,3,2,0:T(2,128)}, u32[]{:S(2)}) copy-start(s32[1,16,4,2]{1,3,2,0:T(2,128)} %param.18) | copy-start | bytes 1540
  43.4 3.2 %copy-start.8 = (bf16[128,128]{1,0:T(8,128)(2,1)S(1)}, bf16[128,128]{1,0:T(8,128)(2,1)}, u32[]{:S(2)}) copy-start(bf16[128,128]{1,0:T(8,128)(2,1)} %constant.24.clone.pick_ref) | copy-start | bytes 98308
  43.4 3.2 %copy-start.9 = (bf16[64,128]{1,0:T(8,128)(2,1)S(1)}, bf16[64,128]{1,0:T(8,128)(2,1)}, u32[]{:S(2)}) copy-start(bf16[64,128]{1,0:T(8,128)(2,1)} %constant.22.clone.place_ref) | copy-start | bytes 49156
  43.4 3.2 %copy-start.10 = (s32[32,128]{1,0:T(8,128)S(1)}, s32[32,128]{1,0:T(8,128)}, u32[]{:S(2)}) copy-start(s32[32,128]{1,0:T(8,128)} %constant.23.clone.owner_ref) | copy-start | bytes 49156
  46.6 1.6 %copy-start = (f32[16,2,4,32,32]{4,3,2,1,0:T(8,128)S(1)}, f32[16,2,4,32,32]{4,3,2,1,0:T(8,128)}, u32[]{:S(2)}) copy-start(f32[16,2,4,32,32]{4,3,2,1,0:T(8,128)} %reshape.35.diag_ref) | copy-start | bytes 1572868
  48.1 1.4 %copy-start.1 = (f32[16,2,3,32,32]{4,3,2,1,0:T(8,128)S(1)}, f32[16,2,3,32,32]{4,3,2,1,0:T(8,128)}, u32[]{:S(2)}) copy-start(f32[16,2,3,32,32]{4,3,2,1,0:T(8,128)} %copy.21.off_ref) | copy-start | bytes 1179652
  53.1 29.4 %copy-start.2 = (bf16[4,256,512]{2,1,0:T(8,128)(2,1)S(1)}, bf16[4,256,512]{2,1,0:T(8,128)(2,1)}, u32[]{:S(2)}) copy-start(bf16[4,256,512]{2,1,0:T(8,128)(2,1)} %constant.29.clone.high_ref) | copy-start | bytes 3145732
  53.1 29.4 %copy-start.3 = (bf16[4,256,512]{2,1,0:T(8,128)(2,1)S(1)}, bf16[4,256,512]{2,1,0:T(8,128)(2,1)}, u32[]{:S(2)}) copy-start(bf16[4,256,512]{2,1,0:T(8,128)(2,1)} %constant.30.clone.low_ref) | copy-start | bytes 3145732
  82.5 18.3 %copy-start.6 = (bf16[2,256,256]{2,1,0:T(8,128)(2,1)S(1)}, bf16[2,256,256]{2,1,0:T(8,128)(2,1)}, u32[]{:S(2)}) copy-start(bf16[2,256,256]{2,1,0:T(8,128)(2,1)} %constant.31.clone.high_ref) | copy-start | bytes 786436
  82.5 18.3 %copy-start.7 = (bf16[2,256,256]{2,1,0:T(8,128)(2,1)S(1)}, bf16[2,256,256]{2,1,0:T(8,128)(2,1)}, u32[]{:S(2)}) copy-start(bf16[2,256,256]{2,1,0:T(8,128)(2,1)} %constant.32.clone.low_ref) | copy-start | bytes 786436

commit v3 on v2

--- a/solution.py
+++ b/solution.py
@@ -56,28 +56,30 @@
     return split_table(forward), split_table(backward)
 
 
-def slab_order(count):
-    levels = count // 4
-    return [
-        (high * levels + (levels - 2 - i) % levels) * 2 + core
-        for high in (1, 0)
-        for core in (1, 0)
-        for i in range(levels)
-    ]
-
-
-def line_order():
-    return [4 * y + x for x in (1, 3, 2, 0) for y in (2, 1, 0, 3)]
-
-
-def order_tables(order):
-    count = len(order)
-    lane = np.arange(4 * count)
-    index = 4 * np.array(order)[lane % count] + lane // count
+def slab_order(highs, cores, levels):
+    return [(8 * high + z) * 2 + core for high in highs for core in cores for z in levels]
+
+
+def line_order(along_x, along_y):
+    return [4 * y + x for x in along_x for y in along_y]
+
+
+SLABS_THERE = slab_order((1, 0), (1, 0), (7, 6, 5, 4, 3, 2, 1, 0))
+SLABS_BACK = slab_order((1, 0), (1, 0), (6, 5, 4, 3, 2, 1, 0, 7))
+LINES_THERE = line_order((2, 1, 3, 0), (1, 2, 3, 0))
+LINES_BACK = line_order((1, 3, 2, 0), (2, 1, 0, 3))
+
+
+def operator_tables(there, back):
+    def levels(order):
+        lane = np.arange(4 * len(order))
+        return 4 * np.array(order)[lane % len(order)] + lane // len(order)
+
+    column, line = levels(there), levels(back)
     row = np.arange(BLOCK).reshape(BLOCK, 1)
-    place = np.tile(index % BLOCK == row, (2, 1)).astype(ml_dtypes.bfloat16)
-    owner = np.broadcast_to(index // BLOCK, (BLOCK, 4 * count)).astype(np.int32)
-    pick = (index.reshape(-1, 1) == lane).astype(ml_dtypes.bfloat16)
+    place = np.tile(column % BLOCK == row, (2, 1)).astype(ml_dtypes.bfloat16)
+    owner = np.broadcast_to(column // BLOCK, (BLOCK, len(column))).astype(np.int32)
+    pick = (line.reshape(-1, 1) == np.arange(len(line))).astype(ml_dtypes.bfloat16)
     return place, owner, pick
 
 
@@ -320,8 +322,6 @@
     groups = operator_blocks.shape[1]
     forward_x, backward_x = x_tables()
     forward_y, backward_y = y_tables()
-    order = slab_order(32)
-    line = line_order()
     square = (BLOCK, BLOCK)
     operator = call(
         operator_kernel,
@@ -330,7 +330,7 @@
         operator_blocks.reshape((groups, 4, 2) + square),
         diag_inverse.reshape((groups, 2, 4) + square),
         off_blocks.reshape((groups, 2, 3) + square),
-        *order_tables(order),
+        *operator_tables(SLABS_THERE, SLABS_BACK),
         dtype=bf16,
         spaces=[pltpu.SMEM] + [None] * 6,
         scratch=[pltpu.VMEM((groups, LANES, LANES), f32)],
@@ -339,7 +339,7 @@
     x_flops = 2 * 3 * depth * lines * length * HALF
     y_flops = 2 * 3 * 4 * QUARTER * 2 * QUARTER * LANES
     values = call(
-        functools.partial(x_forward_kernel, line),
+        functools.partial(x_forward_kernel, LINES_THERE),
         (16, lines, LANES),
         grid_field,
         *forward_x,
@@ -352,11 +352,11 @@
         ],
         flops=x_flops,
     )
-    values = exchange(values, "gx", line).reshape(NY, LANES)
+    values = exchange(values, "gx", LINES_THERE).reshape(NY, LANES)
     values = call(
-        functools.partial(y_kernel, 1.0, line, order), (NY, LANES), values, *forward_y, flops=y_flops
-    )
-    values = exchange(values.reshape(32, 32, LANES), "gy", order).reshape(NY, LANES)
+        functools.partial(y_kernel, 1.0, LINES_THERE, SLABS_THERE), (NY, LANES), values, *forward_y, flops=y_flops
+    )
+    values = exchange(values.reshape(32, 32, LANES), "gy", SLABS_THERE).reshape(NY, LANES)
     values = call(
         apply_kernel,
         (NY, LANES),
@@ -364,13 +364,13 @@
         operator,
         flops=2 * 3 * groups * LANES * LANES * LANES,
     )
-    values = exchange(values.reshape(32, 32, LANES), "gy", order).reshape(NY, LANES)
+    values = exchange(values.reshape(32, 32, LANES), "gy", SLABS_BACK).reshape(NY, LANES)
     values = call(
-        functools.partial(y_kernel, -1.0, order, line), (NY, LANES), values, *backward_y, flops=y_flops
-    )
-    values = exchange(values.reshape(16, lines, LANES), "gx", line)
+        functools.partial(y_kernel, -1.0, SLABS_BACK, LINES_BACK), (NY, LANES), values, *backward_y, flops=y_flops
+    )
+    values = exchange(values.reshape(16, lines, LANES), "gx", LINES_BACK)
     return call(
-        functools.partial(x_backward_kernel, line),
+        functools.partial(x_backward_kernel, LINES_BACK),
         (depth, lines, length),
         values,
         *backward_x,

time: 103 us -> 103 us (level)
  starting transfers between devices: 19.3 us -> 17.9 us
    all_to_all x1, starting transfers between devices: 19.3 us -> 17.9 us  [exchange(): lax.all_to_all(values, axis, split_axis=0, concat_axis=0, axis_index_grou...]
where the time goes in v3:
time: 103 us; the launch traced here: 102 us
  blocking collectives  60.9 us (59%)
  starting transfers between devices  17.9 us (17%)
  Pallas kernels  11.8 us (11%)
  local copies, waits for them, and re-layouts  8.2 us (8%)
  waiting for transfers between devices  3.17 us (3%)
    all_to_all x3, blocking collectives, exchange(): lax.all_to_all(values, axis, split_axis=0, concat_axis=0, axis_index_grou...  60.9 us
    all_to_all x1, starting transfers between devices, exchange(): lax.all_to_all(values, axis, split_axis=0, concat_axis=0, axis_index_grou...  17.9 us
    pallas_call x6, Pallas kernels, call(): pl.pallas_call(kernel, out_shape=jax.ShapeDtypeStruct(shape, dtype), in_s...  11.8 us
    unnamed x30, local copies, waits for them, and re-layouts  3.19 us
    all_to_all x1, waiting for transfers between devices, exchange(): lax.all_to_all(values, axis, split_axis=0, concat_axis=0, axis_index_grou...  3.17 us
  transfers between devices with their start and end apart: 1, of which 1 were waited for; matrix products, arithmetic and copies ran while one was open for 5% of the time, Pallas kernels for 3%

profile of v3, /device:TPU:1, one launch (start us, length us, event | category | flops | bytes accessed | tf_op | source)
XLA Modules:
  0.0 102.1 jit_solution(4381033605588087410)
XLA Ops:
  0.0 0.0 copy-start.4
  0.0 0.0 copy-start.5
  0.0 2.1 %shard_map.154 = f32[16,64,128]{2,1,0:T(8,128)S(1)} custom-call(f32[4,64,512]{2,1,0:T(8,128)} %grid_hbm.1, bf16[2,256,256]{2,1,0:T(8,128)(2,1)} %constant.25.clone.high_hbm, bf16[2,256,256]{2,1,0:T(8,128)(2,1)} %constant.26.clone.low_hbm), custom_call_target="tpu_custom_call" | custom-call | flops 201326592 | bytes 1048576 | tf_op jit(solution)/shard_map/pallas_call | solution.py:302
  2.1 20.2 %all_to_all.20 = f32[16,64,128]{2,1,0:T(8,128)S(1)} all-to-all(f32[16,64,128]{2,1,0:T(8,128)S(1)} %shard_map.154), channel_id=1, replica_groups={{192,320,448,64,160,288,416,32,224,352,480,96,128,256,384,0},{193,321,4..., dimensions={0} | all-to-all | bytes 1048576 | tf_op jit(solution)/shard_map/all_to_all | solution.py:315
  22.3 0.0 copy-done.4
  22.3 0.0 copy-done.5
  22.4 0.0 copy-start.13
  22.4 1.6 %shard_map.155 = f32[1024,128]{1,0:T(8,128)} custom-call(f32[1024,128]{1,0:T(8,128)S(1)} %bitcast.9, bf16[4,256,512]{2,1,0:T(8,128)(2,1)S(1)} %copy-done.4, bf16[4,256,512]{2,1,0:T(8,128)(2,1)S(1)} %copy-done.5), custom_call_target="tpu_custom_call" | custom-call | flops 402653184 | bytes 2621440 | tf_op jit(solution)/shard_map/pallas_call | solution.py:302
  24.0 17.9 %all-to-all-start.1 = ((f32[32,32,128]{2,1,0:T(8,128)}), f32[32,32,128]{2,1,0:T(8,128)}, u32[]{:S(2)}, u32[]{:S(2)}) async-start(f32[32,32,128]{2,1,0:T(8,128)} %bitcast.1), calls=%async_computation.1 | async-start | bytes 1048576 | tf_op jit(solution)/shard_map/all_to_all | solution.py:315
  41.9 0.0 copy-done.13
  41.9 0.0 copy-start.11
  42.0 0.7 reshape.40
  42.6 1.3 %copy.21.off_ref = f32[16,2,3,32,32]{4,3,2,1,0:T(8,128)} copy(f32[16,2,3,32,32]{4,3,1,2,0:T(8,128)S(1)} %reshape.40) | data formatting | bytes 786432 | tf_op jit(solution)/shard_map/reshape | solution.py:332
  44.0 0.0 copy-done.11
  44.0 0.0 copy-start.12
  44.0 0.0 copy-start.14
  44.0 0.0 copy-start.8
  44.0 0.0 copy-start.9
  44.0 0.0 copy-start.10
  44.0 0.9 reshape.34.blocks_ref
  44.9 0.1 copy-done.12
  45.0 2.0 %reshape.35.diag_ref = f32[16,2,4,32,32]{4,3,2,1,0:T(8,128)} reshape(f32[1,16,2,4,1024]{4,3,2,1,0:T(4,128)S(1)} %copy-done.12) | data formatting | bytes 1048576 | tf_op jit(solution)/shard_map/reshape | solution.py:331
  47.1 0.0 copy-done.14
  47.1 0.1 copy.20.columns_ref
  47.2 0.0 copy-done.8
  47.2 0.0 copy-done.9
  47.2 0.0 copy-done.10
  47.2 0.0 copy-start
  47.2 1.6 %copy-done = f32[16,2,4,32,32]{4,3,2,1,0:T(8,128)S(1)} copy-done((f32[16,2,4,32,32]{4,3,2,1,0:T(8,128)S(1)}, f32[16,2,4,32,32]{4,3,2,1,0:T(8,128)}, u32[]{:S(2)}) %copy-start) | copy-done | bytes 524312
  48.8 0.0 copy-start.1
  48.8 1.4 %copy-done.1 = f32[16,2,3,32,32]{4,3,2,1,0:T(8,128)S(1)} copy-done((f32[16,2,3,32,32]{4,3,2,1,0:T(8,128)S(1)}, f32[16,2,3,32,32]{4,3,2,1,0:T(8,128)}, u32[]{:S(2)}) %copy-start.1) | copy-done | bytes 393240
  50.2 3.5 %shard_map.156.operator_ref = bf16[16,128,256]{2,1,0:T(8,128)(2,1)S(1)} custom-call(s32[16,8]{1,0:T(8,128)S(1)} %copy.20.columns_ref, f32[16,4,2,32,32]{4,3,2,1,0:T(8,128)S(1)} %reshape.34.blocks_ref, f32[16,2,4,32,32]{4,3,2,1,0:T(8,128)S(1)} %copy-done, f32[16,2,3,32,32]{4,3,2,1,0:T(8,128)S(1)} %copy-done.1, bf16[64,128]{1,0:T(8,128)(2,1)S(1)} %copy-done.9, ...), custom_call_target="tpu_custom_call" | custom-call | flops 276824064 | bytes 1507840 | tf_op jit(solution)/shard_map/pallas_call | solution.py:302
  53.7 0.0 copy-start.2
  53.7 0.0 copy-start.3
  53.7 3.2 %all-to-all-done.1 = f32[32,32,128]{2,1,0:T(8,128)} async-done(((f32[32,32,128]{2,1,0:T(8,128)}), f32[32,32,128]{2,1,0:T(8,128)}, u32[]{:S(2)}, u32[]{:S(2)}) %all-to-all-start.1) | async-done | bytes 524320 | tf_op jit(solution)/shard_map/all_to_all | solution.py:315
  56.9 2.2 %shard_map.157 = f32[1024,128]{1,0:T(8,128)S(1)} custom-call(f32[1024,128]{1,0:T(8,128)} %bitcast.2.in_ref, bf16[16,128,256]{2,1,0:T(8,128)(2,1)S(1)} %shard_map.156.operator_ref), custom_call_target="tpu_custom_call" | custom-call | flops 201326592 | bytes 1572864 | tf_op jit(solution)/shard_map/pallas_call | solution.py:302
  59.1 24.7 %all_to_all.21 = f32[32,32,128]{2,1,0:T(8,128)S(1)} all-to-all(f32[32,32,128]{2,1,0:T(8,128)S(1)} %bitcast.12), channel_id=1, replica_groups={{29,27,25,23,21,19,17,31,28,26,24,22,20,18,16,30,13,11,9,7,5,3,1,15,12,..., dimensions={0} | all-to-all | bytes 1048576 | tf_op jit(solution)/shard_map/all_to_all | solution.py:315
  83.8 0.0 copy-done.2
  83.8 0.0 copy-done.3
  83.8 0.0 copy-start.6
  83.9 0.0 copy-start.7
  83.9 0.8 shard_map.158
  84.7 16.0 %all_to_all.22.in_ref = f32[16,64,128]{2,1,0:T(8,128)S(1)} all-to-all(f32[16,64,128]{2,1,0:T(8,128)S(1)} %bitcast.11), channel_id=1, replica_groups={{288,160,32,416,352,224,96,480,320,192,64,448,256,128,0,384},{289,161,3..., dimensions={0} | all-to-all | bytes 1048576 | tf_op jit(solution)/shard_map/all_to_all | solution.py:315
  100.7 0.0 copy-done.6
  100.7 0.0 copy-done.7
  100.7 1.4 %shard_map.159 = f32[4,64,512]{2,1,0:T(8,128)} custom-call(f32[16,64,128]{2,1,0:T(8,128)S(1)} %all_to_all.22.in_ref, bf16[2,256,256]{2,1,0:T(8,128)(2,1)S(1)} %copy-done.6, bf16[2,256,256]{2,1,0:T(8,128)(2,1)S(1)} %copy-done.7), custom_call_target="tpu_custom_call" | custom-call | flops 201326592 | bytes 1048576 | tf_op jit(solution)/shard_map/pallas_call | solution.py:302
Async XLA Ops:
  0.0 22.3 %copy-start.4 = (bf16[4,256,512]{2,1,0:T(8,128)(2,1)S(1)}, bf16[4,256,512]{2,1,0:T(8,128)(2,1)}, u32[]{:S(2)}) copy-start(bf16[4,256,512]{2,1,0:T(8,128)(2,1)} %constant.27.clone.high_ref) | copy-start | bytes 3145732
  0.0 22.3 %copy-start.5 = (bf16[4,256,512]{2,1,0:T(8,128)(2,1)S(1)}, bf16[4,256,512]{2,1,0:T(8,128)(2,1)}, u32[]{:S(2)}) copy-start(bf16[4,256,512]{2,1,0:T(8,128)(2,1)} %constant.28.clone.low_ref) | copy-start | bytes 3145732
  22.4 19.6 %copy-start.13 = (f32[1,16,2,3,1024]{4,2,3,1,0:T(2,128)S(1)}, f32[1,16,2,3,1024]{4,2,3,1,0:T(2,128)}, u32[]{:S(2)}) copy-start(f32[1,16,2,3,1024]{4,2,3,1,0:T(2,128)} %param.20) | copy-start | bytes 1179652
  24.0 32.9 %all-to-all-start.1 = ((f32[32,32,128]{2,1,0:T(8,128)}), f32[32,32,128]{2,1,0:T(8,128)}, u32[]{:S(2)}, u32[]{:S(2)}) async-start(f32[32,32,128]{2,1,0:T(8,128)} %bitcast.1), calls=%async_computation.1 | async-start | bytes 1048576 | tf_op jit(solution)/shard_map/all_to_all | solution.py:315
  41.9 2.0 %copy-start.11 = (f32[1,16,4,2,1024]{4,3,2,1,0:T(2,128)S(1)}, f32[1,16,4,2,1024]{4,3,2,1,0:T(2,128)}, u32[]{:S(2)}) copy-start(f32[1,16,4,2,1024]{4,3,2,1,0:T(2,128)} %param.17) | copy-start | bytes 1572868
  44.0 1.0 %copy-start.12 = (f32[1,16,2,4,1024]{4,3,2,1,0:T(4,128)S(1)}, f32[1,16,2,4,1024]{4,3,2,1,0:T(4,128)}, u32[]{:S(2)}) copy-start(f32[1,16,2,4,1024]{4,3,2,1,0:T(4,128)} %param.19) | copy-start | bytes 1572868
  44.0 3.1 %copy-start.14 = (s32[1,16,4,2]{1,3,2,0:T(2,128)S(1)}, s32[1,16,4,2]{1,3,2,0:T(2,128)}, u32[]{:S(2)}) copy-start(s32[1,16,4,2]{1,3,2,0:T(2,128)} %param.18) | copy-start | bytes 1540
  44.0 3.2 %copy-start.8 = (bf16[128,128]{1,0:T(8,128)(2,1)S(1)}, bf16[128,128]{1,0:T(8,128)(2,1)}, u32[]{:S(2)}) copy-start(bf16[128,128]{1,0:T(8,128)(2,1)} %constant.24.clone.pick_ref) | copy-start | bytes 98308
  44.0 3.2 %copy-start.9 = (bf16[64,128]{1,0:T(8,128)(2,1)S(1)}, bf16[64,128]{1,0:T(8,128)(2,1)}, u32[]{:S(2)}) copy-start(bf16[64,128]{1,0:T(8,128)(2,1)} %constant.22.clone.place_ref) | copy-start | bytes 49156
  44.0 3.2 %copy-start.10 = (s32[32,128]{1,0:T(8,128)S(1)}, s32[32,128]{1,0:T(8,128)}, u32[]{:S(2)}) copy-start(s32[32,128]{1,0:T(8,128)} %constant.23.clone.owner_ref) | copy-start | bytes 49156
  47.2 1.6 %copy-start = (f32[16,2,4,32,32]{4,3,2,1,0:T(8,128)S(1)}, f32[16,2,4,32,32]{4,3,2,1,0:T(8,128)}, u32[]{:S(2)}) copy-start(f32[16,2,4,32,32]{4,3,2,1,0:T(8,128)} %reshape.35.diag_ref) | copy-start | bytes 1572868
  48.8 1.4 %copy-start.1 = (f32[16,2,3,32,32]{4,3,2,1,0:T(8,128)S(1)}, f32[16,2,3,32,32]{4,3,2,1,0:T(8,128)}, u32[]{:S(2)}) copy-start(f32[16,2,3,32,32]{4,3,2,1,0:T(8,128)} %copy.21.off_ref) | copy-start | bytes 1179652
  53.7 30.2 %copy-start.2 = (bf16[4,256,512]{2,1,0:T(8,128)(2,1)S(1)}, bf16[4,256,512]{2,1,0:T(8,128)(2,1)}, u32[]{:S(2)}) copy-start(bf16[4,256,512]{2,1,0:T(8,128)(2,1)} %constant.29.clone.high_ref) | copy-start | bytes 3145732
  53.7 30.1 %copy-start.3 = (bf16[4,256,512]{2,1,0:T(8,128)(2,1)S(1)}, bf16[4,256,512]{2,1,0:T(8,128)(2,1)}, u32[]{:S(2)}) copy-start(bf16[4,256,512]{2,1,0:T(8,128)(2,1)} %constant.30.clone.low_ref) | copy-start | bytes 3145732
  83.8 16.8 %copy-start.6 = (bf16[2,256,256]{2,1,0:T(8,128)(2,1)S(1)}, bf16[2,256,256]{2,1,0:T(8,128)(2,1)}, u32[]{:S(2)}) copy-start(bf16[2,256,256]{2,1,0:T(8,128)(2,1)} %constant.31.clone.high_ref) | copy-start | bytes 786436
  83.9 16.8 %copy-start.7 = (bf16[2,256,256]{2,1,0:T(8,128)(2,1)S(1)}, bf16[2,256,256]{2,1,0:T(8,128)(2,1)}, u32[]{:S(2)}) copy-start(bf16[2,256,256]{2,1,0:T(8,128)(2,1)} %constant.32.clone.low_ref) | copy-start | bytes 786436

commit v4 on v3

--- a/solution.py
+++ b/solution.py
@@ -67,7 +67,7 @@
 SLABS_THERE = slab_order((1, 0), (1, 0), (7, 6, 5, 4, 3, 2, 1, 0))
 SLABS_BACK = slab_order((1, 0), (1, 0), (6, 5, 4, 3, 2, 1, 0, 7))
 LINES_THERE = line_order((2, 1, 3, 0), (1, 2, 3, 0))
-LINES_BACK = line_order((1, 3, 2, 0), (2, 1, 0, 3))
+LINES_BACK = line_order((2, 1, 3, 0), (1, 2, 3, 0))
 
 
 def operator_tables(there, back):

time: 103 us -> 104 us (level)
  blocking collectives: 60.9 us -> 62.5 us
    all_to_all x3, blocking collectives: 60.9 us -> 62.5 us  [exchange(): lax.all_to_all(values, axis, split_axis=0, concat_axis=0, axis_index_grou...]
where the time goes in v4:
time: 104 us
  blocking collectives  62.5 us (60%)
  starting transfers between devices  17.9 us (17%)
  Pallas kernels  11.8 us (11%)
  local copies, waits for them, and re-layouts  8.2 us (8%)
  waiting for transfers between devices  3.17 us (3%)
    all_to_all x3, blocking collectives, exchange(): lax.all_to_all(values, axis, split_axis=0, concat_axis=0, axis_index_grou...  62.5 us
    all_to_all x1, starting transfers between devices, exchange(): lax.all_to_all(values, axis, split_axis=0, concat_axis=0, axis_index_grou...  17.9 us
    pallas_call x6, Pallas kernels, call(): pl.pallas_call(kernel, out_shape=jax.ShapeDtypeStruct(shape, dtype), in_s...  11.8 us
    unnamed x30, local copies, waits for them, and re-layouts  3.19 us
    all_to_all x1, waiting for transfers between devices, exchange(): lax.all_to_all(values, axis, split_axis=0, concat_axis=0, axis_index_grou...  3.17 us
  transfers between devices with their start and end apart: 1, of which 1 were waited for; matrix products, arithmetic and copies ran while one was open for 5% of the time, Pallas kernels for 3%

profile of v4, /device:TPU:1, one launch (start us, length us, event | category | flops | bytes accessed | tf_op | source)
XLA Modules:
  0.0 103.7 jit_solution(1720087430218202537)
XLA Ops:
  0.0 0.0 copy-start.4
  0.0 0.0 copy-start.5
  0.0 2.1 %shard_map.154 = f32[16,64,128]{2,1,0:T(8,128)S(1)} custom-call(f32[4,64,512]{2,1,0:T(8,128)} %grid_hbm.1, bf16[2,256,256]{2,1,0:T(8,128)(2,1)} %constant.25.clone.high_hbm, bf16[2,256,256]{2,1,0:T(8,128)(2,1)} %constant.26.clone.low_hbm), custom_call_target="tpu_custom_call" | custom-call | flops 201326592 | bytes 1048576 | tf_op jit(solution)/shard_map/pallas_call | solution.py:302
  2.1 20.2 %all_to_all.20 = f32[16,64,128]{2,1,0:T(8,128)S(1)} all-to-all(f32[16,64,128]{2,1,0:T(8,128)S(1)} %shard_map.154), channel_id=1, replica_groups={{192,320,448,64,160,288,416,32,224,352,480,96,128,256,384,0},{193,321,4..., dimensions={0} | all-to-all | bytes 1048576 | tf_op jit(solution)/shard_map/all_to_all | solution.py:315
  22.3 0.0 copy-done.4
  22.3 0.0 copy-done.5
  22.4 0.0 copy-start.13
  22.4 1.6 %shard_map.155 = f32[1024,128]{1,0:T(8,128)} custom-call(f32[1024,128]{1,0:T(8,128)S(1)} %bitcast.9, bf16[4,256,512]{2,1,0:T(8,128)(2,1)S(1)} %copy-done.4, bf16[4,256,512]{2,1,0:T(8,128)(2,1)S(1)} %copy-done.5), custom_call_target="tpu_custom_call" | custom-call | flops 402653184 | bytes 2621440 | tf_op jit(solution)/shard_map/pallas_call | solution.py:302
  24.0 17.9 %all-to-all-start.1 = ((f32[32,32,128]{2,1,0:T(8,128)}), f32[32,32,128]{2,1,0:T(8,128)}, u32[]{:S(2)}, u32[]{:S(2)}) async-start(f32[32,32,128]{2,1,0:T(8,128)} %bitcast.1), calls=%async_computation.1 | async-start | bytes 1048576 | tf_op jit(solution)/shard_map/all_to_all | solution.py:315
  41.9 0.0 copy-done.13
  41.9 0.0 copy-start.11
  42.0 0.7 reshape.40
  42.6 1.3 %copy.21.off_ref = f32[16,2,3,32,32]{4,3,2,1,0:T(8,128)} copy(f32[16,2,3,32,32]{4,3,1,2,0:T(8,128)S(1)} %reshape.40) | data formatting | bytes 786432 | tf_op jit(solution)/shard_map/reshape | solution.py:332
  44.0 0.0 copy-done.11
  44.0 0.0 copy-start.12
  44.0 0.0 copy-start.14
  44.0 0.0 copy-start.8
  44.0 0.0 copy-start.9
  44.0 0.0 copy-start.10
  44.0 0.9 reshape.34.blocks_ref
  44.9 0.1 copy-done.12
  45.0 2.0 %reshape.35.diag_ref = f32[16,2,4,32,32]{4,3,2,1,0:T(8,128)} reshape(f32[1,16,2,4,1024]{4,3,2,1,0:T(4,128)S(1)} %copy-done.12) | data formatting | bytes 1048576 | tf_op jit(solution)/shard_map/reshape | solution.py:331
  47.1 0.0 copy-done.14
  47.1 0.1 copy.20.columns_ref
  47.2 0.0 copy-done.8
  47.2 0.0 copy-done.9
  47.2 0.0 copy-done.10
  47.2 0.0 copy-start
  47.2 1.6 %copy-done = f32[16,2,4,32,32]{4,3,2,1,0:T(8,128)S(1)} copy-done((f32[16,2,4,32,32]{4,3,2,1,0:T(8,128)S(1)}, f32[16,2,4,32,32]{4,3,2,1,0:T(8,128)}, u32[]{:S(2)}) %copy-start) | copy-done | bytes 524312
  48.8 0.0 copy-start.1
  48.8 1.4 %copy-done.1 = f32[16,2,3,32,32]{4,3,2,1,0:T(8,128)S(1)} copy-done((f32[16,2,3,32,32]{4,3,2,1,0:T(8,128)S(1)}, f32[16,2,3,32,32]{4,3,2,1,0:T(8,128)}, u32[]{:S(2)}) %copy-start.1) | copy-done | bytes 393240
  50.2 3.5 %shard_map.156.operator_ref = bf16[16,128,256]{2,1,0:T(8,128)(2,1)S(1)} custom-call(s32[16,8]{1,0:T(8,128)S(1)} %copy.20.columns_ref, f32[16,4,2,32,32]{4,3,2,1,0:T(8,128)S(1)} %reshape.34.blocks_ref, f32[16,2,4,32,32]{4,3,2,1,0:T(8,128)S(1)} %copy-done, f32[16,2,3,32,32]{4,3,2,1,0:T(8,128)S(1)} %copy-done.1, bf16[64,128]{1,0:T(8,128)(2,1)S(1)} %copy-done.9, ...), custom_call_target="tpu_custom_call" | custom-call | flops 276824064 | bytes 1507840 | tf_op jit(solution)/shard_map/pallas_call | solution.py:302
  53.7 0.0 copy-start.2
  53.7 0.0 copy-start.3
  53.7 3.2 %all-to-all-done.1 = f32[32,32,128]{2,1,0:T(8,128)} async-done(((f32[32,32,128]{2,1,0:T(8,128)}), f32[32,32,128]{2,1,0:T(8,128)}, u32[]{:S(2)}, u32[]{:S(2)}) %all-to-all-start.1) | async-done | bytes 524320 | tf_op jit(solution)/shard_map/all_to_all | solution.py:315
  56.9 2.2 %shard_map.157 = f32[1024,128]{1,0:T(8,128)S(1)} custom-call(f32[1024,128]{1,0:T(8,128)} %bitcast.2.in_ref, bf16[16,128,256]{2,1,0:T(8,128)(2,1)S(1)} %shard_map.156.operator_ref), custom_call_target="tpu_custom_call" | custom-call | flops 201326592 | bytes 1572864 | tf_op jit(solution)/shard_map/pallas_call | solution.py:302
  59.1 24.7 %all_to_all.21 = f32[32,32,128]{2,1,0:T(8,128)S(1)} all-to-all(f32[32,32,128]{2,1,0:T(8,128)S(1)} %bitcast.12), channel_id=1, replica_groups={{29,27,25,23,21,19,17,31,28,26,24,22,20,18,16,30,13,11,9,7,5,3,1,15,12,..., dimensions={0} | all-to-all | bytes 1048576 | tf_op jit(solution)/shard_map/all_to_all | solution.py:315
  83.8 0.0 copy-done.2
  83.8 0.0 copy-done.3
  83.8 0.0 copy-start.6
  83.9 0.0 copy-start.7
  83.9 0.8 shard_map.158
  84.7 17.6 %all_to_all.22.in_ref = f32[16,64,128]{2,1,0:T(8,128)S(1)} all-to-all(f32[16,64,128]{2,1,0:T(8,128)S(1)} %bitcast.11), channel_id=1, replica_groups={{192,320,448,64,160,288,416,32,224,352,480,96,128,256,384,0},{193,321,4..., dimensions={0} | all-to-all | bytes 1048576 | tf_op jit(solution)/shard_map/all_to_all | solution.py:315
  102.3 0.0 copy-done.6
  102.3 0.0 copy-done.7
  102.3 1.4 %shard_map.159 = f32[4,64,512]{2,1,0:T(8,128)} custom-call(f32[16,64,128]{2,1,0:T(8,128)S(1)} %all_to_all.22.in_ref, bf16[2,256,256]{2,1,0:T(8,128)(2,1)S(1)} %copy-done.6, bf16[2,256,256]{2,1,0:T(8,128)(2,1)S(1)} %copy-done.7), custom_call_target="tpu_custom_call" | custom-call | flops 201326592 | bytes 1048576 | tf_op jit(solution)/shard_map/pallas_call | solution.py:302
Async XLA Ops:
  0.0 22.3 %copy-start.4 = (bf16[4,256,512]{2,1,0:T(8,128)(2,1)S(1)}, bf16[4,256,512]{2,1,0:T(8,128)(2,1)}, u32[]{:S(2)}) copy-start(bf16[4,256,512]{2,1,0:T(8,128)(2,1)} %constant.27.clone.high_ref) | copy-start | bytes 3145732
  0.0 22.3 %copy-start.5 = (bf16[4,256,512]{2,1,0:T(8,128)(2,1)S(1)}, bf16[4,256,512]{2,1,0:T(8,128)(2,1)}, u32[]{:S(2)}) copy-start(bf16[4,256,512]{2,1,0:T(8,128)(2,1)} %constant.28.clone.low_ref) | copy-start | bytes 3145732
  22.4 19.6 %copy-start.13 = (f32[1,16,2,3,1024]{4,2,3,1,0:T(2,128)S(1)}, f32[1,16,2,3,1024]{4,2,3,1,0:T(2,128)}, u32[]{:S(2)}) copy-start(f32[1,16,2,3,1024]{4,2,3,1,0:T(2,128)} %param.20) | copy-start | bytes 1179652
  24.0 32.9 %all-to-all-start.1 = ((f32[32,32,128]{2,1,0:T(8,128)}), f32[32,32,128]{2,1,0:T(8,128)}, u32[]{:S(2)}, u32[]{:S(2)}) async-start(f32[32,32,128]{2,1,0:T(8,128)} %bitcast.1), calls=%async_computation.1 | async-start | bytes 1048576 | tf_op jit(solution)/shard_map/all_to_all | solution.py:315
  41.9 2.0 %copy-start.11 = (f32[1,16,4,2,1024]{4,3,2,1,0:T(2,128)S(1)}, f32[1,16,4,2,1024]{4,3,2,1,0:T(2,128)}, u32[]{:S(2)}) copy-start(f32[1,16,4,2,1024]{4,3,2,1,0:T(2,128)} %param.17) | copy-start | bytes 1572868
  44.0 1.0 %copy-start.12 = (f32[1,16,2,4,1024]{4,3,2,1,0:T(4,128)S(1)}, f32[1,16,2,4,1024]{4,3,2,1,0:T(4,128)}, u32[]{:S(2)}) copy-start(f32[1,16,2,4,1024]{4,3,2,1,0:T(4,128)} %param.19) | copy-start | bytes 1572868
  44.0 3.1 %copy-start.14 = (s32[1,16,4,2]{1,3,2,0:T(2,128)S(1)}, s32[1,16,4,2]{1,3,2,0:T(2,128)}, u32[]{:S(2)}) copy-start(s32[1,16,4,2]{1,3,2,0:T(2,128)} %param.18) | copy-start | bytes 1540
  44.0 3.2 %copy-start.8 = (bf16[128,128]{1,0:T(8,128)(2,1)S(1)}, bf16[128,128]{1,0:T(8,128)(2,1)}, u32[]{:S(2)}) copy-start(bf16[128,128]{1,0:T(8,128)(2,1)} %constant.24.clone.pick_ref) | copy-start | bytes 98308
  44.0 3.2 %copy-start.9 = (bf16[64,128]{1,0:T(8,128)(2,1)S(1)}, bf16[64,128]{1,0:T(8,128)(2,1)}, u32[]{:S(2)}) copy-start(bf16[64,128]{1,0:T(8,128)(2,1)} %constant.22.clone.place_ref) | copy-start | bytes 49156
  44.0 3.2 %copy-start.10 = (s32[32,128]{1,0:T(8,128)S(1)}, s32[32,128]{1,0:T(8,128)}, u32[]{:S(2)}) copy-start(s32[32,128]{1,0:T(8,128)} %constant.23.clone.owner_ref) | copy-start | bytes 49156
  47.2 1.6 %copy-start = (f32[16,2,4,32,32]{4,3,2,1,0:T(8,128)S(1)}, f32[16,2,4,32,32]{4,3,2,1,0:T(8,128)}, u32[]{:S(2)}) copy-start(f32[16,2,4,32,32]{4,3,2,1,0:T(8,128)} %reshape.35.diag_ref) | copy-start | bytes 1572868
  48.8 1.4 %copy-start.1 = (f32[16,2,3,32,32]{4,3,2,1,0:T(8,128)S(1)}, f32[16,2,3,32,32]{4,3,2,1,0:T(8,128)}, u32[]{:S(2)}) copy-start(f32[16,2,3,32,32]{4,3,2,1,0:T(8,128)} %copy.21.off_ref) | copy-start | bytes 1179652
  53.7 30.2 %copy-start.2 = (bf16[4,256,512]{2,1,0:T(8,128)(2,1)S(1)}, bf16[4,256,512]{2,1,0:T(8,128)(2,1)}, u32[]{:S(2)}) copy-start(bf16[4,256,512]{2,1,0:T(8,128)(2,1)} %constant.29.clone.high_ref) | copy-start | bytes 3145732
  53.7 30.1 %copy-start.3 = (bf16[4,256,512]{2,1,0:T(8,128)(2,1)S(1)}, bf16[4,256,512]{2,1,0:T(8,128)(2,1)}, u32[]{:S(2)}) copy-start(bf16[4,256,512]{2,1,0:T(8,128)(2,1)} %constant.30.clone.low_ref) | copy-start | bytes 3145732
  83.8 18.5 %copy-start.6 = (bf16[2,256,256]{2,1,0:T(8,128)(2,1)S(1)}, bf16[2,256,256]{2,1,0:T(8,128)(2,1)}, u32[]{:S(2)}) copy-start(bf16[2,256,256]{2,1,0:T(8,128)(2,1)} %constant.31.clone.high_ref) | copy-start | bytes 786436
  83.9 18.5 %copy-start.7 = (bf16[2,256,256]{2,1,0:T(8,128)(2,1)S(1)}, bf16[2,256,256]{2,1,0:T(8,128)(2,1)}, u32[]{:S(2)}) copy-start(bf16[2,256,256]{2,1,0:T(8,128)(2,1)} %constant.32.clone.low_ref) | copy-start | bytes 786436

commit v5 on v3

--- a/solution.py
+++ b/solution.py
@@ -65,7 +65,7 @@
 
 
 SLABS_THERE = slab_order((1, 0), (1, 0), (7, 6, 5, 4, 3, 2, 1, 0))
-SLABS_BACK = slab_order((1, 0), (1, 0), (6, 5, 4, 3, 2, 1, 0, 7))
+SLABS_BACK = slab_order((1, 0), (1, 0), (7, 0, 1, 2, 3, 4, 5, 6))
 LINES_THERE = line_order((2, 1, 3, 0), (1, 2, 3, 0))
 LINES_BACK = line_order((1, 3, 2, 0), (2, 1, 0, 3))
 

time: 103 us -> 103 us (level)
  no operation moved by 1% of the time
where the time goes in v5:
time: 103 us; the launch traced here: 102 us
  blocking collectives  61 us (59%)
  starting transfers between devices  17.9 us (17%)
  Pallas kernels  11.8 us (11%)
  local copies, waits for them, and re-layouts  8.2 us (8%)
  waiting for transfers between devices  3.17 us (3%)
    all_to_all x3, blocking collectives, exchange(): lax.all_to_all(values, axis, split_axis=0, concat_axis=0, axis_index_grou...  61 us
    all_to_all x1, starting transfers between devices, exchange(): lax.all_to_all(values, axis, split_axis=0, concat_axis=0, axis_index_grou...  17.9 us
    pallas_call x6, Pallas kernels, call(): pl.pallas_call(kernel, out_shape=jax.ShapeDtypeStruct(shape, dtype), in_s...  11.8 us
    unnamed x30, local copies, waits for them, and re-layouts  3.19 us
    all_to_all x1, waiting for transfers between devices, exchange(): lax.all_to_all(values, axis, split_axis=0, concat_axis=0, axis_index_grou...  3.17 us
  transfers between devices with their start and end apart: 1, of which 1 were waited for; matrix products, arithmetic and copies ran while one was open for 5% of the time, Pallas kernels for 3%

profile of v5, /device:TPU:1, one launch (start us, length us, event | category | flops | bytes accessed | tf_op | source)
XLA Modules:
  0.0 102.3 jit_solution(6973626414773594003)
XLA Ops:
  0.0 0.0 copy-start.4
  0.0 0.0 copy-start.5
  0.0 2.1 %shard_map.154 = f32[16,64,128]{2,1,0:T(8,128)S(1)} custom-call(f32[4,64,512]{2,1,0:T(8,128)} %grid_hbm.1, bf16[2,256,256]{2,1,0:T(8,128)(2,1)} %constant.25.clone.high_hbm, bf16[2,256,256]{2,1,0:T(8,128)(2,1)} %constant.26.clone.low_hbm), custom_call_target="tpu_custom_call" | custom-call | flops 201326592 | bytes 1048576 | tf_op jit(solution)/shard_map/pallas_call | solution.py:302
  2.1 20.2 %all_to_all.20 = f32[16,64,128]{2,1,0:T(8,128)S(1)} all-to-all(f32[16,64,128]{2,1,0:T(8,128)S(1)} %shard_map.154), channel_id=1, replica_groups={{192,320,448,64,160,288,416,32,224,352,480,96,128,256,384,0},{193,321,4..., dimensions={0} | all-to-all | bytes 1048576 | tf_op jit(solution)/shard_map/all_to_all | solution.py:315
  22.3 0.0 copy-done.4
  22.3 0.0 copy-done.5
  22.4 0.0 copy-start.13
  22.4 1.6 %shard_map.155 = f32[1024,128]{1,0:T(8,128)} custom-call(f32[1024,128]{1,0:T(8,128)S(1)} %bitcast.9, bf16[4,256,512]{2,1,0:T(8,128)(2,1)S(1)} %copy-done.4, bf16[4,256,512]{2,1,0:T(8,128)(2,1)S(1)} %copy-done.5), custom_call_target="tpu_custom_call" | custom-call | flops 402653184 | bytes 2621440 | tf_op jit(solution)/shard_map/pallas_call | solution.py:302
  24.0 17.9 %all-to-all-start.1 = ((f32[32,32,128]{2,1,0:T(8,128)}), f32[32,32,128]{2,1,0:T(8,128)}, u32[]{:S(2)}, u32[]{:S(2)}) async-start(f32[32,32,128]{2,1,0:T(8,128)} %bitcast.1), calls=%async_computation.1 | async-start | bytes 1048576 | tf_op jit(solution)/shard_map/all_to_all | solution.py:315
  41.9 0.0 copy-done.13
  41.9 0.0 copy-start.11
  42.0 0.7 reshape.40
  42.6 1.3 %copy.21.off_ref = f32[16,2,3,32,32]{4,3,2,1,0:T(8,128)} copy(f32[16,2,3,32,32]{4,3,1,2,0:T(8,128)S(1)} %reshape.40) | data formatting | bytes 786432 | tf_op jit(solution)/shard_map/reshape | solution.py:332
  44.0 0.0 copy-done.11
  44.0 0.0 copy-start.12
  44.0 0.0 copy-start.14
  44.0 0.0 copy-start.8
  44.0 0.0 copy-start.9
  44.0 0.0 copy-start.10
  44.0 0.9 reshape.34.blocks_ref
  44.9 0.1 copy-done.12
  45.0 2.0 %reshape.35.diag_ref = f32[16,2,4,32,32]{4,3,2,1,0:T(8,128)} reshape(f32[1,16,2,4,1024]{4,3,2,1,0:T(4,128)S(1)} %copy-done.12) | data formatting | bytes 1048576 | tf_op jit(solution)/shard_map/reshape | solution.py:331
  47.1 0.0 copy-done.14
  47.1 0.1 copy.20.columns_ref
  47.2 0.0 copy-done.8
  47.2 0.0 copy-done.9
  47.2 0.0 copy-done.10
  47.2 0.0 copy-start
  47.2 1.6 %copy-done = f32[16,2,4,32,32]{4,3,2,1,0:T(8,128)S(1)} copy-done((f32[16,2,4,32,32]{4,3,2,1,0:T(8,128)S(1)}, f32[16,2,4,32,32]{4,3,2,1,0:T(8,128)}, u32[]{:S(2)}) %copy-start) | copy-done | bytes 524312
  48.8 0.0 copy-start.1
  48.8 1.4 %copy-done.1 = f32[16,2,3,32,32]{4,3,2,1,0:T(8,128)S(1)} copy-done((f32[16,2,3,32,32]{4,3,2,1,0:T(8,128)S(1)}, f32[16,2,3,32,32]{4,3,2,1,0:T(8,128)}, u32[]{:S(2)}) %copy-start.1) | copy-done | bytes 393240
  50.2 3.5 %shard_map.156.operator_ref = bf16[16,128,256]{2,1,0:T(8,128)(2,1)S(1)} custom-call(s32[16,8]{1,0:T(8,128)S(1)} %copy.20.columns_ref, f32[16,4,2,32,32]{4,3,2,1,0:T(8,128)S(1)} %reshape.34.blocks_ref, f32[16,2,4,32,32]{4,3,2,1,0:T(8,128)S(1)} %copy-done, f32[16,2,3,32,32]{4,3,2,1,0:T(8,128)S(1)} %copy-done.1, bf16[64,128]{1,0:T(8,128)(2,1)S(1)} %copy-done.9, ...), custom_call_target="tpu_custom_call" | custom-call | flops 276824064 | bytes 1507840 | tf_op jit(solution)/shard_map/pallas_call | solution.py:302
  53.7 0.0 copy-start.2
  53.7 0.0 copy-start.3
  53.7 3.2 %all-to-all-done.1 = f32[32,32,128]{2,1,0:T(8,128)} async-done(((f32[32,32,128]{2,1,0:T(8,128)}), f32[32,32,128]{2,1,0:T(8,128)}, u32[]{:S(2)}, u32[]{:S(2)}) %all-to-all-start.1) | async-done | bytes 524320 | tf_op jit(solution)/shard_map/all_to_all | solution.py:315
  56.9 2.2 %shard_map.157 = f32[1024,128]{1,0:T(8,128)S(1)} custom-call(f32[1024,128]{1,0:T(8,128)} %bitcast.2.in_ref, bf16[16,128,256]{2,1,0:T(8,128)(2,1)S(1)} %shard_map.156.operator_ref), custom_call_target="tpu_custom_call" | custom-call | flops 201326592 | bytes 1572864 | tf_op jit(solution)/shard_map/pallas_call | solution.py:302
  59.1 24.7 %all_to_all.21 = f32[32,32,128]{2,1,0:T(8,128)S(1)} all-to-all(f32[32,32,128]{2,1,0:T(8,128)S(1)} %bitcast.12), channel_id=1, replica_groups={{31,17,19,21,23,25,27,29,30,16,18,20,22,24,26,28,15,1,3,5,7,9,11,13,14,..., dimensions={0} | all-to-all | bytes 1048576 | tf_op jit(solution)/shard_map/all_to_all | solution.py:315
  83.8 0.0 copy-done.2
  83.8 0.0 copy-done.3
  83.8 0.0 copy-start.6
  83.8 0.0 copy-start.7
  83.8 0.8 shard_map.158
  84.7 16.2 %all_to_all.22.in_ref = f32[16,64,128]{2,1,0:T(8,128)S(1)} all-to-all(f32[16,64,128]{2,1,0:T(8,128)S(1)} %bitcast.11), channel_id=1, replica_groups={{288,160,32,416,352,224,96,480,320,192,64,448,256,128,0,384},{289,161,3..., dimensions={0} | all-to-all | bytes 1048576 | tf_op jit(solution)/shard_map/all_to_all | solution.py:315
  100.8 0.0 copy-done.6
  100.9 0.0 copy-done.7
  100.9 1.4 %shard_map.159 = f32[4,64,512]{2,1,0:T(8,128)} custom-call(f32[16,64,128]{2,1,0:T(8,128)S(1)} %all_to_all.22.in_ref, bf16[2,256,256]{2,1,0:T(8,128)(2,1)S(1)} %copy-done.6, bf16[2,256,256]{2,1,0:T(8,128)(2,1)S(1)} %copy-done.7), custom_call_target="tpu_custom_call" | custom-call | flops 201326592 | bytes 1048576 | tf_op jit(solution)/shard_map/pallas_call | solution.py:302
Async XLA Ops:
  0.0 22.3 %copy-start.4 = (bf16[4,256,512]{2,1,0:T(8,128)(2,1)S(1)}, bf16[4,256,512]{2,1,0:T(8,128)(2,1)}, u32[]{:S(2)}) copy-start(bf16[4,256,512]{2,1,0:T(8,128)(2,1)} %constant.27.clone.high_ref) | copy-start | bytes 3145732
  0.0 22.3 %copy-start.5 = (bf16[4,256,512]{2,1,0:T(8,128)(2,1)S(1)}, bf16[4,256,512]{2,1,0:T(8,128)(2,1)}, u32[]{:S(2)}) copy-start(bf16[4,256,512]{2,1,0:T(8,128)(2,1)} %constant.28.clone.low_ref) | copy-start | bytes 3145732
  22.4 19.6 %copy-start.13 = (f32[1,16,2,3,1024]{4,2,3,1,0:T(2,128)S(1)}, f32[1,16,2,3,1024]{4,2,3,1,0:T(2,128)}, u32[]{:S(2)}) copy-start(f32[1,16,2,3,1024]{4,2,3,1,0:T(2,128)} %param.20) | copy-start | bytes 1179652
  24.0 32.9 %all-to-all-start.1 = ((f32[32,32,128]{2,1,0:T(8,128)}), f32[32,32,128]{2,1,0:T(8,128)}, u32[]{:S(2)}, u32[]{:S(2)}) async-start(f32[32,32,128]{2,1,0:T(8,128)} %bitcast.1), calls=%async_computation.1 | async-start | bytes 1048576 | tf_op jit(solution)/shard_map/all_to_all | solution.py:315
  41.9 2.0 %copy-start.11 = (f32[1,16,4,2,1024]{4,3,2,1,0:T(2,128)S(1)}, f32[1,16,4,2,1024]{4,3,2,1,0:T(2,128)}, u32[]{:S(2)}) copy-start(f32[1,16,4,2,1024]{4,3,2,1,0:T(2,128)} %param.17) | copy-start | bytes 1572868
  44.0 1.0 %copy-start.12 = (f32[1,16,2,4,1024]{4,3,2,1,0:T(4,128)S(1)}, f32[1,16,2,4,1024]{4,3,2,1,0:T(4,128)}, u32[]{:S(2)}) copy-start(f32[1,16,2,4,1024]{4,3,2,1,0:T(4,128)} %param.19) | copy-start | bytes 1572868
  44.0 3.1 %copy-start.14 = (s32[1,16,4,2]{1,3,2,0:T(2,128)S(1)}, s32[1,16,4,2]{1,3,2,0:T(2,128)}, u32[]{:S(2)}) copy-start(s32[1,16,4,2]{1,3,2,0:T(2,128)} %param.18) | copy-start | bytes 1540
  44.0 3.2 %copy-start.8 = (bf16[128,128]{1,0:T(8,128)(2,1)S(1)}, bf16[128,128]{1,0:T(8,128)(2,1)}, u32[]{:S(2)}) copy-start(bf16[128,128]{1,0:T(8,128)(2,1)} %constant.24.clone.pick_ref) | copy-start | bytes 98308
  44.0 3.2 %copy-start.9 = (bf16[64,128]{1,0:T(8,128)(2,1)S(1)}, bf16[64,128]{1,0:T(8,128)(2,1)}, u32[]{:S(2)}) copy-start(bf16[64,128]{1,0:T(8,128)(2,1)} %constant.22.clone.place_ref) | copy-start | bytes 49156
  44.0 3.2 %copy-start.10 = (s32[32,128]{1,0:T(8,128)S(1)}, s32[32,128]{1,0:T(8,128)}, u32[]{:S(2)}) copy-start(s32[32,128]{1,0:T(8,128)} %constant.23.clone.owner_ref) | copy-start | bytes 49156
  47.2 1.6 %copy-start = (f32[16,2,4,32,32]{4,3,2,1,0:T(8,128)S(1)}, f32[16,2,4,32,32]{4,3,2,1,0:T(8,128)}, u32[]{:S(2)}) copy-start(f32[16,2,4,32,32]{4,3,2,1,0:T(8,128)} %reshape.35.diag_ref) | copy-start | bytes 1572868
  48.8 1.4 %copy-start.1 = (f32[16,2,3,32,32]{4,3,2,1,0:T(8,128)S(1)}, f32[16,2,3,32,32]{4,3,2,1,0:T(8,128)}, u32[]{:S(2)}) copy-start(f32[16,2,3,32,32]{4,3,2,1,0:T(8,128)} %copy.21.off_ref) | copy-start | bytes 1179652
  53.7 30.1 %copy-start.2 = (bf16[4,256,512]{2,1,0:T(8,128)(2,1)S(1)}, bf16[4,256,512]{2,1,0:T(8,128)(2,1)}, u32[]{:S(2)}) copy-start(bf16[4,256,512]{2,1,0:T(8,128)(2,1)} %constant.29.clone.high_ref) | copy-start | bytes 3145732
  53.7 30.1 %copy-start.3 = (bf16[4,256,512]{2,1,0:T(8,128)(2,1)S(1)}, bf16[4,256,512]{2,1,0:T(8,128)(2,1)}, u32[]{:S(2)}) copy-start(bf16[4,256,512]{2,1,0:T(8,128)(2,1)} %constant.30.clone.low_ref) | copy-start | bytes 3145732
  83.8 17.0 %copy-start.6 = (bf16[2,256,256]{2,1,0:T(8,128)(2,1)S(1)}, bf16[2,256,256]{2,1,0:T(8,128)(2,1)}, u32[]{:S(2)}) copy-start(bf16[2,256,256]{2,1,0:T(8,128)(2,1)} %constant.31.clone.high_ref) | copy-start | bytes 786436
  83.8 17.0 %copy-start.7 = (bf16[2,256,256]{2,1,0:T(8,128)(2,1)S(1)}, bf16[2,256,256]{2,1,0:T(8,128)(2,1)}, u32[]{:S(2)}) copy-start(bf16[2,256,256]{2,1,0:T(8,128)(2,1)} %constant.32.clone.low_ref) | copy-start | bytes 786436
